TPU v7x, 32 devices: a whole 2x2x4 slice. The times are simulated.
32 devices in a mesh: grp: 1, date: 16 (over z, y, x), tile: 2 (over core).
Axes of the slice: x: 2, y: 2, z: 4, core: 2. Of those that a mesh axis runs over, the one named last changes fastest.
Arguments:
- acquisitions: bfloat16 [2, 64, 32, 8192], P(None, 'date', 'grp', 'tile'), may hold values from -102 to 102
- pair_list: int32 [960, 2], P('date'), may hold values from -1 to 63, as said below
- win_rows: int32 [8], replicated, may hold values from 1 to 8
- win_cols: int32 [1], replicated, may hold values from 18 to 32
Outputs:
- coherence: float32 [2, 960, 8, 512], P(None, 'date', 'grp', 'tile')
Inputs may be any that keep to these rules, and one draw needn't show every extreme that they name: `pair_list`: the 60 slots of one owner (one index of date) list pairs (i, j) whose first date i is held by that owner, with i < j <= i + 15; each pair stands once; live slots come first and unused slots hold -1 in both columns; some owner has all slots live.
All inputs are finite; a program needn't handle non-finite values.
Results may differ from a plain program's by a relative error of at most 0.0013.
Values may be sent and summed in bfloat16 or wider, within the bound.
A program may use at most 64 MiB of HBM per device.

v0:
```python
import math

import jax
import jax.numpy as jnp
from jax import lax
from jax.sharding import PartitionSpec as P

SPAN = 15
STRIDE_R = 4
STRIDE_C = 16


EPS = 1e-06


def partner(value, axis, distance):
    mask = 2**distance
    pairs = [(source, source ^ mask) for source in range(lax.axis_size(axis))]
    return lax.ppermute(value, axis, pairs)


def from_behind(block, axis, distance):
    devices = range(lax.axis_size(axis))
    route = [(i - distance, i) for i in devices if i - distance in devices]
    return lax.ppermute(block, axis, route)


def column_taps(width, lead_cols, out_count, win_cols):
    in_index = lax.broadcasted_iota(jnp.int32, (width, out_count), 0)
    out_index = lax.broadcasted_iota(jnp.int32, (width, out_count), 1)
    distance = jnp.abs(2 * (in_index - lead_cols) + 1 - (2 * out_index + 1) * STRIDE_C)
    return (distance <= win_cols[0]).astype(jnp.bfloat16)


def partial_sums(window, pairs, start_date, taps_rows, col_taps, group_size):
    real_part = window[0].astype(jnp.float32)
    imag_part = window[1].astype(jnp.float32)
    power_map = (real_part * real_part + imag_part * imag_part).astype(jnp.bfloat16)
    power_cols = jnp.einsum("drc,ck->drk", power_map, col_taps, preferred_element_type=jnp.float32)
    looked_power = jnp.einsum("or,drk->dok", taps_rows, power_cols, precision=lax.Precision.HIGHEST)
    window_dates = window.shape[1]
    pair_count = pairs.shape[0]
    live_count = jnp.sum((pairs[:, 0] >= 0).astype(jnp.int32))
    block_total = (live_count + group_size - 1) // group_size

    def one_block(block_index, buffer):
        block_start = block_index * group_size
        chosen = lax.dynamic_slice_in_dim(pairs, block_start, group_size, 0)
        first_local = jnp.clip(chosen[:, 0] - start_date, 0, window_dates - 1)
        second_local = jnp.clip(chosen[:, 1] - start_date, 0, window_dates - 1)
        lead_tile = jnp.take(window, first_local, axis=1).astype(jnp.float32)
        other_tile = jnp.take(window, second_local, axis=1).astype(jnp.float32)
        product = jnp.stack(
            (
                lead_tile[0] * other_tile[0] + lead_tile[1] * other_tile[1],
                lead_tile[1] * other_tile[0] - lead_tile[0] * other_tile[1],
            )
        ).astype(jnp.bfloat16)
        across = jnp.einsum("cprx,xk->cprk", product, col_taps, preferred_element_type=jnp.float32)
        looked = jnp.einsum("or,cprk->cpok", taps_rows, across, precision=lax.Precision.HIGHEST)
        return lax.dynamic_update_slice_in_dim(buffer, looked, block_start, 1)

    initial = jnp.zeros((2, pair_count, taps_rows.shape[0], col_taps.shape[1]), jnp.float32)
    return (looked_power, lax.fori_loop(0, block_total, one_block, initial))


def shards(acquisitions, pair_list, win_rows, win_cols):
    date_count = acquisitions.shape[1]
    row_count = acquisitions.shape[2]
    col_count = acquisitions.shape[3]
    out_rows = row_count // STRIDE_R
    out_cols = col_count // STRIDE_C
    half_cols = STRIDE_C // 2
    reach_devices = (date_count - 1 + SPAN) // date_count
    own_index = lax.axis_index("date")
    own_start = own_index * date_count
    tile_index = lax.axis_index("tile")
    outgoing = jnp.where(
        tile_index == 0, acquisitions[..., col_count - half_cols :], acquisitions[..., :half_cols]
    )
    incoming = partner(outgoing, "tile", 0)
    nothing = jnp.zeros_like(incoming)
    lower_rim = jnp.where(tile_index == 1, incoming, nothing)
    upper_rim = jnp.where(tile_index == 0, incoming, nothing)
    local_block = jnp.concatenate((lower_rim, acquisitions, upper_rim), axis=3)
    col_taps = column_taps(col_count + 2 * half_cols, half_cols, out_cols, win_cols)
    out_index = lax.broadcasted_iota(jnp.int32, (out_rows, row_count), 0)
    row_index = lax.broadcasted_iota(jnp.int32, (out_rows, row_count), 1)
    row_taps = (
        jnp.abs(2 * row_index + 1 - (2 * out_index + 1) * STRIDE_R) <= win_rows[:, None]
    ).astype(jnp.float32)
    pair_count = pair_list.shape[0]
    group_size = math.gcd(pair_count, 8)
    pieces = [local_block]
    for distance in range(1, reach_devices + 1):
        pieces.append(from_behind(local_block, "date", -distance))
    window = jnp.concatenate(pieces, axis=1)
    looked_power, looked_all = partial_sums(
        window, pair_list, own_start, row_taps, col_taps, group_size
    )
    window_dates = looked_power.shape[0]
    live_count = jnp.sum((pair_list[:, 0] >= 0).astype(jnp.int32))
    block_total = (live_count + group_size - 1) // group_size

    def finish_block(block_index, result):
        block_start = block_index * group_size
        chosen = lax.dynamic_slice_in_dim(pair_list, block_start, group_size, 0)
        alive_mask = chosen[:, 0] >= 0
        first_local = jnp.clip(chosen[:, 0] - own_start, 0, window_dates - 1)
        second_local = jnp.clip(chosen[:, 1] - own_start, 0, window_dates - 1)
        looked = lax.dynamic_slice_in_dim(looked_all, block_start, group_size, 1)
        power_first = jnp.take(looked_power, first_local, axis=0)
        power_second = jnp.take(looked_power, second_local, axis=0)
        denominator = jnp.sqrt(power_first * power_second + EPS)
        coherent = jnp.where(alive_mask[None, :, None, None], looked / denominator[None], 0.0)
        return lax.dynamic_update_slice_in_dim(result, coherent, block_start, 1)

    initial = jnp.zeros((2, pair_count, out_rows, out_cols), jnp.float32)
    return lax.fori_loop(0, block_total, finish_block, initial)


def solution(mesh):
    return jax.shard_map(
        shards,
        mesh=mesh,
        in_specs=(P(None, "date", "grp", "tile"), P("date", None), P(), P()),
        out_specs=P(None, "date", "grp", "tile"),
        check_vma=False,
    )
```

profile of v0, /device:TPU:0, one launch (start us, length us, event | category | flops | bytes accessed | tf_op | source)
XLA Modules:
  0.0 548.2 jit_solution(260910387351198371)
XLA Ops:
  14.4 44.8 %collective-permute-done.1 = bf16[2,4,32,4112]{3,2,1,0:T(8,128)(2,1)} collective-permute-done((bf16[2,4,32,4112]{3,2,1,0:T(8,128)(2,1)S(1)}, bf16[2,4,32,4112]{3,2,1,0:T(8,128)(2,1)}, u32[]{:S(2)}, u32[]{:S(2)}) %collective-permute-start.1) | collective-permute-done | bytes 2105376 | tf_op jit(solution)/shard_map/ppermute | solution.py:25
  61.1 47.5 %collective-permute-done.2 = bf16[2,4,32,4112]{3,2,1,0:T(8,128)(2,1)} collective-permute-done((bf16[2,4,32,4112]{3,2,1,0:T(8,128)(2,1)S(1)}, bf16[2,4,32,4112]{3,2,1,0:T(8,128)(2,1)}, u32[]{:S(2)}, u32[]{:S(2)}) %collective-permute-start.2) | collective-permute-done | bytes 2105376 | tf_op jit(solution)/shard_map/ppermute | solution.py:25
  112.5 161.6 %collective-permute-done.4 = bf16[2,4,32,4112]{3,2,1,0:T(8,128)(2,1)S(1)} collective-permute-done((bf16[2,4,32,4112]{3,2,1,0:T(8,128)(2,1)S(1)}, bf16[2,4,32,4112]{3,2,1,0:T(8,128)(2,1)S(1)}, u32[]{:S(2)}, u32[]{:S(2)}) %collective-permute-start.4) | collective-permute-done | bytes 2105376 | tf_op jit(solution)/shard_map/ppermute | solution.py:25
  278.4 240.5 %while.22 = (s32[]{:T(128)}, f32[2,60,8,256]{3,2,1,0:T(8,128)S(1)}, s32[]{:T(128)}, s32[60,2]{0,1:T(2,128)S(1)}, s32[]{:T(128)}, /*index=5*/bf16[2,20,32,4112]{3...) while((s32[]{:T(128)}, f32[2,60,8,256]{3,2,1,0:T(8,128)S(1)}, ...), condition=%wide.region_2.4_spmd.clone, body=%wide.region_1.3_spmd.clone.sunk | while | flops 558947392 | bytes 34302948 | solution.py:64
  278.6 4.9 gather_fusion.2
  283.5 6.2 %gather_fusion.3 = bf16[4,2,32,4112]{3,2,1,0:T(8,128)(2,1)} fusion(bf16[2,20,32,4112]{3,2,1,0:T(8,128)(2,1)} %get-tuple-element.365, s32[1024]{0:T(1024)S(1)} %pad_clamp_fusion.9), kind=kCustom, calls=%fused_computation.clone.clone.1 | custom fusion | bytes 4210704 | tf_op jit(solution)/shard_map/while/body/jit(_take)/gather | solution.py:51
  294.6 4.9 gather_fusion.2
  299.5 6.2 %gather_fusion.3 = bf16[4,2,32,4112]{3,2,1,0:T(8,128)(2,1)} fusion(bf16[2,20,32,4112]{3,2,1,0:T(8,128)(2,1)} %get-tuple-element.365, s32[1024]{0:T(1024)S(1)} %pad_clamp_fusion.9), kind=kCustom, calls=%fused_computation.clone.clone.1 | custom fusion | bytes 4210704 | tf_op jit(solution)/shard_map/while/body/jit(_take)/gather | solution.py:51
  310.6 4.9 gather_fusion.2
  315.6 6.2 %gather_fusion.3 = bf16[4,2,32,4112]{3,2,1,0:T(8,128)(2,1)} fusion(bf16[2,20,32,4112]{3,2,1,0:T(8,128)(2,1)} %get-tuple-element.365, s32[1024]{0:T(1024)S(1)} %pad_clamp_fusion.9), kind=kCustom, calls=%fused_computation.clone.clone.1 | custom fusion | bytes 4210704 | tf_op jit(solution)/shard_map/while/body/jit(_take)/gather | solution.py:51
  326.7 4.9 gather_fusion.2
  331.6 6.2 %gather_fusion.3 = bf16[4,2,32,4112]{3,2,1,0:T(8,128)(2,1)} fusion(bf16[2,20,32,4112]{3,2,1,0:T(8,128)(2,1)} %get-tuple-element.365, s32[1024]{0:T(1024)S(1)} %pad_clamp_fusion.9), kind=kCustom, calls=%fused_computation.clone.clone.1 | custom fusion | bytes 4210704 | tf_op jit(solution)/shard_map/while/body/jit(_take)/gather | solution.py:51
  347.6 6.2 %gather_fusion.3 = bf16[4,2,32,4112]{3,2,1,0:T(8,128)(2,1)} fusion(bf16[2,20,32,4112]{3,2,1,0:T(8,128)(2,1)} %get-tuple-element.365, s32[1024]{0:T(1024)S(1)} %pad_clamp_fusion.9), kind=kCustom, calls=%fused_computation.clone.clone.1 | custom fusion | bytes 4210704 | tf_op jit(solution)/shard_map/while/body/jit(_take)/gather | solution.py:51
  358.7 4.9 gather_fusion.2
  363.7 6.2 %gather_fusion.3 = bf16[4,2,32,4112]{3,2,1,0:T(8,128)(2,1)} fusion(bf16[2,20,32,4112]{3,2,1,0:T(8,128)(2,1)} %get-tuple-element.365, s32[1024]{0:T(1024)S(1)} %pad_clamp_fusion.9), kind=kCustom, calls=%fused_computation.clone.clone.1 | custom fusion | bytes 4210704 | tf_op jit(solution)/shard_map/while/body/jit(_take)/gather | solution.py:51
  374.8 4.9 gather_fusion.2
  379.7 6.2 %gather_fusion.3 = bf16[4,2,32,4112]{3,2,1,0:T(8,128)(2,1)} fusion(bf16[2,20,32,4112]{3,2,1,0:T(8,128)(2,1)} %get-tuple-element.365, s32[1024]{0:T(1024)S(1)} %pad_clamp_fusion.9), kind=kCustom, calls=%fused_computation.clone.clone.1 | custom fusion | bytes 4210704 | tf_op jit(solution)/shard_map/while/body/jit(_take)/gather | solution.py:51
  390.8 4.9 gather_fusion.2
  395.8 6.2 %gather_fusion.3 = bf16[4,2,32,4112]{3,2,1,0:T(8,128)(2,1)} fusion(bf16[2,20,32,4112]{3,2,1,0:T(8,128)(2,1)} %get-tuple-element.365, s32[1024]{0:T(1024)S(1)} %pad_clamp_fusion.9), kind=kCustom, calls=%fused_computation.clone.clone.1 | custom fusion | bytes 4210704 | tf_op jit(solution)/shard_map/while/body/jit(_take)/gather | solution.py:51
  411.8 6.2 %gather_fusion.3 = bf16[4,2,32,4112]{3,2,1,0:T(8,128)(2,1)} fusion(bf16[2,20,32,4112]{3,2,1,0:T(8,128)(2,1)} %get-tuple-element.365, s32[1024]{0:T(1024)S(1)} %pad_clamp_fusion.9), kind=kCustom, calls=%fused_computation.clone.clone.1 | custom fusion | bytes 4210704 | tf_op jit(solution)/shard_map/while/body/jit(_take)/gather | solution.py:51
  422.9 4.9 gather_fusion.2
  427.8 6.2 %gather_fusion.3 = bf16[4,2,32,4112]{3,2,1,0:T(8,128)(2,1)} fusion(bf16[2,20,32,4112]{3,2,1,0:T(8,128)(2,1)} %get-tuple-element.365, s32[1024]{0:T(1024)S(1)} %pad_clamp_fusion.9), kind=kCustom, calls=%fused_computation.clone.clone.1 | custom fusion | bytes 4210704 | tf_op jit(solution)/shard_map/while/body/jit(_take)/gather | solution.py:51
  438.9 4.9 gather_fusion.2
  443.9 6.2 %gather_fusion.3 = bf16[4,2,32,4112]{3,2,1,0:T(8,128)(2,1)} fusion(bf16[2,20,32,4112]{3,2,1,0:T(8,128)(2,1)} %get-tuple-element.365, s32[1024]{0:T(1024)S(1)} %pad_clamp_fusion.9), kind=kCustom, calls=%fused_computation.clone.clone.1 | custom fusion | bytes 4210704 | tf_op jit(solution)/shard_map/while/body/jit(_take)/gather | solution.py:51
  459.9 6.2 %gather_fusion.3 = bf16[4,2,32,4112]{3,2,1,0:T(8,128)(2,1)} fusion(bf16[2,20,32,4112]{3,2,1,0:T(8,128)(2,1)} %get-tuple-element.365, s32[1024]{0:T(1024)S(1)} %pad_clamp_fusion.9), kind=kCustom, calls=%fused_computation.clone.clone.1 | custom fusion | bytes 4210704 | tf_op jit(solution)/shard_map/while/body/jit(_take)/gather | solution.py:51
  475.9 6.2 %gather_fusion.3 = bf16[4,2,32,4112]{3,2,1,0:T(8,128)(2,1)} fusion(bf16[2,20,32,4112]{3,2,1,0:T(8,128)(2,1)} %get-tuple-element.365, s32[1024]{0:T(1024)S(1)} %pad_clamp_fusion.9), kind=kCustom, calls=%fused_computation.clone.clone.1 | custom fusion | bytes 4210704 | tf_op jit(solution)/shard_map/while/body/jit(_take)/gather | solution.py:51
  487.0 4.9 gather_fusion.2
  492.0 6.2 %gather_fusion.3 = bf16[4,2,32,4112]{3,2,1,0:T(8,128)(2,1)} fusion(bf16[2,20,32,4112]{3,2,1,0:T(8,128)(2,1)} %get-tuple-element.365, s32[1024]{0:T(1024)S(1)} %pad_clamp_fusion.9), kind=kCustom, calls=%fused_computation.clone.clone.1 | custom fusion | bytes 4210704 | tf_op jit(solution)/shard_map/while/body/jit(_take)/gather | solution.py:51
  503.1 4.9 gather_fusion.2
  508.0 6.2 %gather_fusion.3 = bf16[4,2,32,4112]{3,2,1,0:T(8,128)(2,1)} fusion(bf16[2,20,32,4112]{3,2,1,0:T(8,128)(2,1)} %get-tuple-element.365, s32[1024]{0:T(1024)S(1)} %pad_clamp_fusion.9), kind=kCustom, calls=%fused_computation.clone.clone.1 | custom fusion | bytes 4210704 | tf_op jit(solution)/shard_map/while/body/jit(_take)/gather | solution.py:51
  519.0 6.7 %fusion.21 = f32[20,32,256]{2,1,0:T(8,128)S(1)} fusion(bf16[2,20,32,4112]{3,2,1,0:T(8,128)(2,1)} %get-tuple-element.409, s32[]{:T(128)} %bitcast.58, s32[256]{0:T(256)S(1)} %get-tuple-element.433, s32[4112]{0:T(1024)S(1)} %get-tuple-element.429), kind=kOutput, calls=%fused_computation.48 | convolution fusion | flops 1366368256 | bytes 11199556 | tf_op jit(solution)/shard_map/drc,ck->drk/dot_general | solution.py:39
  526.1 21.2 %while.21 = (s32[]{:T(128)}, f32[2,60,8,256]{3,2,1,0:T(8,128)S(1)}, s32[]{:T(128)}, s32[60,2]{0,1:T(2,128)S(1)}, f32[2,60,8,256]{3,2,1,0:T(8,128)S(1)}, /*index=...) while((s32[]{:T(128)}, f32[2,60,8,256]{3,2,1,0:T(8,128)S(1)}, ...), condition=%wide.region_4.7_spmd, body=%wide.region_3.6_spmd.sunk | while | flops 67658 | bytes 402315 | solution.py:119
  (275 shorter events, 137.1 us)
Async XLA Ops:
  1.0 1.4 collective-permute-start
  2.4 7.2 %copy-start.2 = (s32[60,2]{0,1:T(2,128)S(1)}, s32[60,2]{0,1:T(2,128)}, u32[]{:S(2)}) copy-start(s32[60,2]{0,1:T(2,128)} %param.13) | copy-start | bytes 1444
  7.0 52.2 %collective-permute-start.1 = (bf16[2,4,32,4112]{3,2,1,0:T(8,128)(2,1)S(1)}, bf16[2,4,32,4112]{3,2,1,0:T(8,128)(2,1)}, u32[]{:S(2)}, u32[]{:S(2)}) collective-permute-start(bf16[2,4,32,4112]{3,2,1,0:T(8,128)(2,1)S(1)} %concatenate.6), channel_id=1, source_target_pairs={{2,0},{4,2},{6,4},{8,6},{10,8},{12,10},{14,12},{16,14},{18,16},{20... | collective-permute-start | bytes 6316040 | tf_op jit(solution)/shard_map/ppermute | solution.py:25
  8.3 100.3 %collective-permute-start.2 = (bf16[2,4,32,4112]{3,2,1,0:T(8,128)(2,1)S(1)}, bf16[2,4,32,4112]{3,2,1,0:T(8,128)(2,1)}, u32[]{:S(2)}, u32[]{:S(2)}) collective-permute-start(bf16[2,4,32,4112]{3,2,1,0:T(8,128)(2,1)S(1)} %concatenate.6), channel_id=1, source_target_pairs={{4,0},{6,2},{8,4},{10,6},{12,8},{14,10},{16,12},{18,14},{20,16},{2... | collective-permute-start | bytes 6316040 | tf_op jit(solution)/shard_map/ppermute | solution.py:25
  10.9 99.6 %collective-permute-start.3 = (bf16[2,4,32,4112]{3,2,1,0:T(8,128)(2,1)S(1)}, bf16[2,4,32,4112]{3,2,1,0:T(8,128)(2,1)}, u32[]{:S(2)}, u32[]{:S(2)}) collective-permute-start(bf16[2,4,32,4112]{3,2,1,0:T(8,128)(2,1)S(1)} %concatenate.6), channel_id=1, source_target_pairs={{6,0},{8,2},{10,4},{12,6},{14,8},{16,10},{18,12},{20,14},{22,16},{... | collective-permute-start | bytes 6316040 | tf_op jit(solution)/shard_map/ppermute | solution.py:25
  12.9 261.1 %collective-permute-start.4 = (bf16[2,4,32,4112]{3,2,1,0:T(8,128)(2,1)S(1)}, bf16[2,4,32,4112]{3,2,1,0:T(8,128)(2,1)S(1)}, u32[]{:S(2)}, u32[]{:S(2)}) collective-permute-start(bf16[2,4,32,4112]{3,2,1,0:T(8,128)(2,1)S(1)} %concatenate.6), channel_id=1, source_target_pairs={{8,0},{10,2},{12,4},{14,6},{16,8},{18,10},{20,12},{22,14},{24,16},... | collective-permute-start | bytes 6316040 | tf_op jit(solution)/shard_map/ppermute | solution.py:25
  112.5 166.0 %copy-start.3 = (s32[8]{0:T(128)S(1)}, s32[8]{0:T(128)}, u32[]{:S(2)}) copy-start(s32[8]{0:T(128)} %param.14) | copy-start | bytes 100
  274.3 4.1 copy-start
  547.3 0.9 copy-start.1
where the time goes:
time: 550 us; the launch traced here: 548 us
  waiting for transfers between devices  255 us (46%)
  local copies, waits for them, and re-layouts  201 us (37%)
  other arithmetic  46.4 us (8%)
  matrix products  36.7 us (7%)
  starting transfers between devices  5.69 us (1%)
    ppermute x4, waiting for transfers between devices, from_behind(): return lax.ppermute(block, axis, route)  254 us
    gather x15, local copies, waits for them, and re-layouts, one_block(): lead_tile = jnp.take(window, first_local, axis=1).astype(jnp.float32)  93.1 us
    gather x15, local copies, waits for them, and re-layouts, one_block(): other_tile = jnp.take(window, second_local, axis=1).astype(jnp.float32)  73.7 us
    convert_element_type x15, other arithmetic, one_block(): other_tile = jnp.take(window, second_local, axis=1).astype(jnp.float32)  33.5 us
    dot_general x15, matrix products, one_block(): jnp.einsum('cprx,xk->cprk', product, col_taps, preferred_element_type=jnp...  25.3 us
  transfers between devices with their start and end apart: 5, of which 4 were waited for; matrix products, arithmetic and copies ran while one was open for 1% of the time, Pallas kernels for 0%

commit v1 on v0

v1 whole, which is shorter than its diff:
```python
import functools

import jax
import jax.numpy as jnp
import numpy as np
from jax import lax
from jax.experimental import pallas as pl
from jax.experimental.pallas import tpu as pltpu
from jax.sharding import PartitionSpec as P

SPAN = 15
STRIDE_R = 4
STRIDE_C = 16
EPS = 1e-06

GROUP = 4
OWN = 4
LOCAL = GROUP * OWN
DOWN = 8
UP_FROM = DOWN + 1
UP = LOCAL - UP_FROM
HELD = LOCAL + DOWN + UP
HALF = STRIDE_C // 2
LANES = 128
CHUNK = 16
MESH = pl.DeviceIdType.MESH


def pair_plan():
    first, second, counts, ups = [], [], [], []
    place = np.zeros((GROUP, OWN * SPAN), np.int32)
    near = [min(SPAN, LOCAL + DOWN - 1 - i) for i in range(LOCAL)]
    for member in range(GROUP):
        at = 0
        for step in range(OWN):
            i = member * OWN + step
            for d in range(near[i]):
                first.append(i)
                second.append(i + 1 + d)
                place[member, step * SPAN + d] = at
                at += 1
        counts.append(at)
        for step in range(OWN):
            i = member * OWN + step
            for d in range(near[i], SPAN):
                place[member, step * SPAN + d] = at
                at += 1
        ups.append(at - counts[-1])
    for member in range(GROUP):
        for step in range(OWN):
            i = member * OWN + step
            for d in range(near[i], SPAN):
                first.append(LOCAL + DOWN + i - UP_FROM)
                second.append(i + 1 + d - LOCAL)
    return np.array(first, np.int32), np.array(second, np.int32), counts, ups, place


FIRST, SECOND, COUNTS, UPS, PLACE = pair_plan()
TOTAL = len(FIRST)
STARTS = [sum(COUNTS[:k]) for k in range(GROUP)]
UP_STARTS = [sum(COUNTS) + sum(UPS[:k]) for k in range(GROUP)]


def other_member(member, k):
    if k == 1:
        return member + 1 - 2 * (member % 2)
    if k == 2:
        return member + 2 - 4 * (member // 2)
    return GROUP - 1 - member


def spread_kernel(groups, width, acq, rim, held, send, recv, far_send, far_recv, local):
    date = lax.axis_index("date")
    group, member = date // GROUP, date % GROUP
    base = group * GROUP
    has_before, has_after = group > 0, group < groups - 1

    barrier = pltpu.get_barrier_semaphore()
    for k in (1, 2, 3):
        pl.semaphore_signal(
            barrier, inc=1, device_id={"date": base + other_member(member, k)}, device_id_type=MESH
        )

    @pl.when(has_before)
    def _():
        pl.semaphore_signal(barrier, inc=1, device_id={"date": date - GROUP}, device_id_type=MESH)

    @pl.when(has_after)
    def _():
        pl.semaphore_signal(barrier, inc=1, device_id={"date": date + GROUP}, device_id_type=MESH)

    peers = GROUP - 1 + has_before.astype(jnp.int32) + has_after.astype(jnp.int32)
    pl.semaphore_wait(barrier, peers)

    def body_of(who):
        return acq.at[:, :, :, pl.ds(pl.multiple_of(who * width, width), width)]

    def rim_of(who):
        return rim.at[who]

    def slot(start, count):
        part = held.at[:, pl.ds(start, count)]
        return part.at[:, :, :, pl.ds(0, width)], part.at[:, :, :, pl.ds(width, LANES)]

    near = []
    for k in (1, 2, 3):
        who = other_member(member, k)
        main, side = slot(member * OWN, OWN)
        pair = [
            pltpu.make_async_remote_copy(
                src_ref=src,
                dst_ref=dst,
                send_sem=send.at[k, n],
                recv_sem=recv.at[k, n],
                device_id={"date": base + who},
                device_id_type=MESH,
            )
            for n, (src, dst) in enumerate(((body_of(who), main), (rim_of(who), side)))
        ]
        for copy in pair:
            copy.start()
        near.append(pair)
    main, side = slot(member * OWN, OWN)
    mine = [
        pltpu.make_async_copy(body_of(member), main, local.at[0]),
        pltpu.make_async_copy(rim_of(member), side, local.at[1]),
    ]
    for copy in mine:
        copy.start()

    onward = [
        (0, OWN, LOCAL, -1),
        (OWN, OWN, LOCAL + OWN, -1),
        (UP_FROM, 3 * OWN - UP_FROM, LOCAL + DOWN, 1),
        (3 * OWN, OWN, LOCAL + DOWN + 3 * OWN - UP_FROM, 1),
    ]

    def far(source):
        start, count, place, step = onward[source]
        return pltpu.make_async_remote_copy(
            src_ref=held.at[:, pl.ds(start, count)],
            dst_ref=held.at[:, pl.ds(place, count)],
            send_sem=far_send.at[source],
            recv_sem=far_recv.at[source],
            device_id={"date": date + step * GROUP},
            device_id_type=MESH,
        )

    def pass_on(who):
        for source in range(GROUP):
            exists = has_before if onward[source][3] < 0 else has_after

            @pl.when(jnp.logical_and(who == source, exists))
            def _():
                far(source).start()

    for copy in mine:
        copy.wait()
    pass_on(member)
    for k in (1, 2, 3):
        for copy in near[k - 1]:
            copy.wait_recv()
        pass_on(other_member(member, k))
    for pair in near:
        for copy in pair:
            copy.wait_send()

    for source in range(GROUP):
        start, count, place, step = onward[source]
        sends = has_before if step < 0 else has_after
        gets = has_after if step < 0 else has_before

        @pl.when(sends)
        def _():
            far(source).wait_send()

        @pl.when(gets)
        def _():
            far(source).wait_recv()

        @pl.when(jnp.logical_not(gets))
        def _():
            fill = pltpu.make_async_copy(
                held.at[:, pl.ds(start, count)], held.at[:, pl.ds(place, count)], local.at[2]
            )
            fill.start()
            fill.wait()


def spread(acq, rim, groups):
    width = acq.shape[3] // GROUP
    return pl.pallas_call(
        functools.partial(spread_kernel, groups, width),
        out_shape=jax.ShapeDtypeStruct((2, HELD, acq.shape[2], width + LANES), acq.dtype),
        in_specs=[pl.BlockSpec(memory_space=pl.ANY)] * 2,
        out_specs=pl.BlockSpec(memory_space=pl.ANY),
        scratch_shapes=[
            pltpu.SemaphoreType.DMA((GROUP, 2)),
            pltpu.SemaphoreType.DMA((GROUP, 2)),
            pltpu.SemaphoreType.DMA((GROUP,)),
            pltpu.SemaphoreType.DMA((GROUP,)),
            pltpu.SemaphoreType.DMA((3,)),
        ],
        compiler_params=pltpu.CompilerParams(collective_id=0, has_side_effects=True),
        name="spread",
    )(acq, rim)


def split_dot(taps, values):
    high = values.astype(jnp.bfloat16)
    low = (values - high.astype(jnp.float32)).astype(jnp.bfloat16)
    return jnp.dot(taps, high, preferred_element_type=jnp.float32) + jnp.dot(
        taps, low, preferred_element_type=jnp.float32
    )


def pairs_kernel(
    rows, width, first, second, win_rows, win_cols, held, result, product, col_taps, row_taps, power
):
    out_rows = rows // STRIDE_R
    out_cols = width // STRIDE_C
    full = width + LANES
    step = pl.program_id(0)
    cuts = [(r, c) for r in range(0, rows, 16) for c in range(0, full, 384)]

    @pl.when(step == 0)
    def _():
        lane = lax.broadcasted_iota(jnp.int32, (full, LANES), 0)
        out = lax.broadcasted_iota(jnp.int32, (full, LANES), 1) % out_cols
        column = jnp.where(
            lane < width, lane, jnp.where(lane < width + HALF, lane - width - HALF, lane - HALF)
        )
        near = jnp.abs(2 * column + 1 - (2 * out + 1) * STRIDE_C) <= win_cols[0]
        near = jnp.logical_and(near, lane < width + 2 * HALF)
        col_taps[...] = jnp.where(near, 1.0, 0.0).astype(jnp.bfloat16)

        shape = (CHUNK * out_rows, CHUNK * rows)
        at = lax.broadcasted_iota(jnp.int32, shape, 0)
        row = lax.broadcasted_iota(jnp.int32, shape, 1)
        window = jnp.zeros(shape, jnp.int32)
        for o in range(out_rows):
            window = jnp.where(at % out_rows == o, win_rows[o], window)
        inside = jnp.abs(2 * (row % rows) + 1 - (2 * (at % out_rows) + 1) * STRIDE_R) <= window
        inside = jnp.logical_and(inside, at // out_rows == row // rows)
        row_taps[...] = jnp.where(inside, 1.0, 0.0).astype(jnp.bfloat16)

        def one_date(d, carry):
            for r, c in cuts:
                re = held[0, d, r : r + 16, c : c + 384].astype(jnp.float32)
                im = held[1, d, r : r + 16, c : c + 384].astype(jnp.float32)
                at = pl.multiple_of(d * rows + r, 16)
                product[pl.ds(at, 16), c : c + 384] = (re * re + im * im).astype(jnp.bfloat16)
            return carry

        lax.fori_loop(0, HELD, one_date, 0)
        product[HELD * rows :] = jnp.zeros((2 * CHUNK * rows - HELD * rows, full), jnp.bfloat16)
        across = jnp.dot(product[...], col_taps[...], preferred_element_type=jnp.float32)
        half = CHUNK * rows
        for n in range(2):
            looked = split_dot(row_taps[...], across[n * half : (n + 1) * half])
            power[n * CHUNK : (n + 1) * CHUNK] = looked.reshape(CHUNK, out_rows, LANES)

    def one_pair(p, carry):
        i = first[step * CHUNK + p]
        j = second[step * CHUNK + p]
        for r, c in cuts:
            re_i = held[0, i, r : r + 16, c : c + 384].astype(jnp.float32)
            im_i = held[1, i, r : r + 16, c : c + 384].astype(jnp.float32)
            re_j = held[0, j, r : r + 16, c : c + 384].astype(jnp.float32)
            im_j = held[1, j, r : r + 16, c : c + 384].astype(jnp.float32)
            at = pl.multiple_of(p * 2 * rows + r, 16)
            product[pl.ds(at, 16), c : c + 384] = (re_i * re_j + im_i * im_j).astype(jnp.bfloat16)
            at = pl.multiple_of(p * 2 * rows + rows + r, 16)
            product[pl.ds(at, 16), c : c + 384] = (im_i * re_j - re_i * im_j).astype(jnp.bfloat16)
        return carry

    lax.fori_loop(0, CHUNK, one_pair, 0)
    across = jnp.dot(product[...], col_taps[...], preferred_element_type=jnp.float32)
    across = across.reshape(CHUNK, 2, rows, LANES)
    lane = lax.broadcasted_iota(jnp.int32, (CHUNK, rows, LANES), 2)
    both = jnp.where(lane < out_cols, across[:, 0], across[:, 1]).reshape(CHUNK * rows, LANES)
    looked = split_dot(row_taps[...], both).reshape(CHUNK, out_rows, LANES)
    for p in range(CHUNK):
        i = first[step * CHUNK + p]
        j = second[step * CHUNK + p]
        result[p] = looked[p] * lax.rsqrt(power[i] * power[j] + EPS)


def work_pairs(held, win_rows, win_cols):
    rows, full = held.shape[2:]
    width = full - LANES
    out_rows = rows // STRIDE_R
    smem = pl.BlockSpec(memory_space=pltpu.SMEM)
    return pl.pallas_call(
        functools.partial(pairs_kernel, rows, width),
        grid=(TOTAL // CHUNK,),
        out_shape=jax.ShapeDtypeStruct((TOTAL, out_rows, LANES), jnp.float32),
        in_specs=[smem, smem, smem, smem, pl.BlockSpec(held.shape, lambda s: (0, 0, 0, 0))],
        out_specs=pl.BlockSpec((CHUNK, out_rows, LANES), lambda s: (s, 0, 0)),
        scratch_shapes=[
            pltpu.VMEM((2 * CHUNK * rows, full), jnp.bfloat16),
            pltpu.VMEM((full, LANES), jnp.bfloat16),
            pltpu.VMEM((CHUNK * out_rows, CHUNK * rows), jnp.bfloat16),
            pltpu.VMEM((2 * CHUNK, out_rows, LANES), jnp.float32),
        ],
        compiler_params=pltpu.CompilerParams(vmem_limit_bytes=48 * 2**20),
        name="work_pairs",
    )(jnp.asarray(FIRST), jnp.asarray(SECOND), win_rows, win_cols, held)


def collect_kernel(groups, result, parts, send, recv, up_send, up_recv, local):
    date = lax.axis_index("date")
    group, member = date // GROUP, date % GROUP
    base = group * GROUP
    has_before, has_after = group > 0, group < groups - 1
    late = [k for k in range(GROUP) if UPS[k]]

    def is_late(who):
        return who >= late[0]

    barrier = pltpu.get_barrier_semaphore()
    for k in (1, 2, 3):
        pl.semaphore_signal(
            barrier, inc=1, device_id={"date": base + other_member(member, k)}, device_id_type=MESH
        )

    @pl.when(has_before)
    def _():
        for k in late:
            pl.semaphore_signal(
                barrier, inc=1, device_id={"date": base - GROUP + k}, device_id_type=MESH
            )

    @pl.when(jnp.logical_and(has_after, is_late(member)))
    def _():
        for k in range(GROUP):
            pl.semaphore_signal(
                barrier, inc=1, device_id={"date": base + GROUP + k}, device_id_type=MESH
            )

    from_after = jnp.logical_and(has_after, is_late(member)).astype(jnp.int32)
    peers = GROUP - 1 + has_before.astype(jnp.int32) * len(late) + from_after * GROUP
    pl.semaphore_wait(barrier, peers)

    def near(source, target):
        return pltpu.make_async_remote_copy(
            src_ref=result.at[pl.ds(STARTS[target], COUNTS[target])],
            dst_ref=parts.at[source, pl.ds(0, COUNTS[target])],
            send_sem=send.at[target],
            recv_sem=recv.at[source],
            device_id={"date": base + target},
            device_id_type=MESH,
        )

    def up(source, target):
        return pltpu.make_async_remote_copy(
            src_ref=result.at[pl.ds(UP_STARTS[target], UPS[target])],
            dst_ref=parts.at[source, pl.ds(COUNTS[target], UPS[target])],
            send_sem=up_send.at[target],
            recv_sem=up_recv.at[source],
            device_id={"date": base - GROUP + target},
            device_id_type=MESH,
        )

    def keep(target):
        return pltpu.make_async_copy(
            result.at[pl.ds(STARTS[target], COUNTS[target])],
            parts.at[target, pl.ds(0, COUNTS[target])],
            local.at[0],
        )

    @pl.when(has_before)
    def _():
        for target in late:
            up(member, target).start()

    for target in range(GROUP):

        @pl.when(member != target)
        def _():
            near(member, target).start()

        @pl.when(member == target)
        def _():
            keep(target).start()

    for target in range(GROUP):

        @pl.when(member != target)
        def _():
            near(member, target).wait_send()

        @pl.when(member == target)
        def _():
            keep(target).wait()
            for source in range(GROUP):
                if source != target:
                    near(source, target).wait_recv()

    @pl.when(has_before)
    def _():
        for target in late:
            up(member, target).wait_send()

    for target in late:

        @pl.when(jnp.logical_and(has_after, member == target))
        def _():
            for source in range(GROUP):
                up(source, target).wait_recv()


def collect(result, groups):
    return pl.pallas_call(
        functools.partial(collect_kernel, groups),
        out_shape=jax.ShapeDtypeStruct((GROUP, OWN * SPAN, *result.shape[1:]), result.dtype),
        in_specs=[pl.BlockSpec(memory_space=pl.ANY)],
        out_specs=pl.BlockSpec(memory_space=pl.ANY),
        scratch_shapes=[pltpu.SemaphoreType.DMA((GROUP,))] * 4 + [pltpu.SemaphoreType.DMA((1,))],
        compiler_params=pltpu.CompilerParams(collective_id=1, has_side_effects=True),
        name="collect",
    )(result)


def slots_kernel(count, pair_list, place, parts, out):
    date = lax.axis_index("date")
    member = date % GROUP
    half = LANES // 2
    left = lax.broadcasted_iota(jnp.int32, (parts.shape[2], LANES), 1) < half

    def one_slot(s, carry):
        i = pair_list[s, 0]
        alive = i >= 0
        at = (i - date * OWN) * SPAN + pair_list[s, 1] - i - 1
        at = jnp.clip(jnp.where(alive, at, 0), 0, OWN * SPAN - 1)
        at = place[member, at]
        for n in range(GROUP // 2):
            a = parts[2 * n, at]
            b = parts[2 * n + 1, at]
            re = jnp.where(left, a, pltpu.roll(b, half, 1))
            im = jnp.where(left, pltpu.roll(a, half, 1), b)
            out[0, s, :, n * LANES : (n + 1) * LANES] = jnp.where(alive, re, 0.0)
            out[1, s, :, n * LANES : (n + 1) * LANES] = jnp.where(alive, im, 0.0)
        return carry

    lax.fori_loop(0, count, one_slot, 0)


def to_slots(pair_list, parts):
    count = pair_list.shape[0]
    smem = pl.BlockSpec(memory_space=pltpu.SMEM)
    vmem = pl.BlockSpec(memory_space=pltpu.VMEM)
    return pl.pallas_call(
        functools.partial(slots_kernel, count),
        out_shape=jax.ShapeDtypeStruct(
            (2, count, parts.shape[2], GROUP * LANES // 2), jnp.float32
        ),
        in_specs=[smem, smem, vmem],
        out_specs=vmem,
        compiler_params=pltpu.CompilerParams(vmem_limit_bytes=16 * 2**20),
        name="to_slots",
    )(pair_list, jnp.asarray(PLACE), parts)


def rims(acq):
    cols = acq.shape[3]
    width = cols // GROUP
    tile = lax.axis_index("tile")
    outgoing = jnp.where(tile == 0, acq[..., cols - HALF :], acq[..., :HALF])
    incoming = lax.ppermute(outgoing, "tile", [(0, 1), (1, 0)])
    nothing = jnp.zeros_like(incoming)
    lower = jnp.where(tile == 1, incoming, nothing)
    upper = jnp.where(tile == 0, incoming, nothing)
    pad = jnp.zeros((*acq.shape[:3], LANES - 2 * HALF), acq.dtype)
    pieces = []
    for k in range(GROUP):
        left = lower if k == 0 else acq[..., k * width - HALF : k * width]
        right = upper if k == GROUP - 1 else acq[..., (k + 1) * width : (k + 1) * width + HALF]
        pieces.append(jnp.concatenate((left, right, pad), axis=3))
    return jnp.stack(pieces)


def shards(groups, acquisitions, pair_list, win_rows, win_cols):
    held = spread(acquisitions, rims(acquisitions), groups)
    result = work_pairs(held, win_rows, win_cols)
    parts = collect(result, groups)
    return to_slots(pair_list, parts)


def solution(mesh):
    return jax.shard_map(
        functools.partial(shards, mesh.shape["date"] // GROUP),
        mesh=mesh,
        in_specs=(P(None, "date", "grp", "tile"), P("date", None), P(), P()),
        out_specs=P(None, "date", "grp", "tile"),
        check_vma=False,
    )
```

time: 550 us -> 150 us (0.27)
  waiting for transfers between devices: 255 us -> 0.01 us
  local copies, waits for them, and re-layouts: 201 us -> 5.3 us
  Pallas kernels: 0 us -> 139 us
  other arithmetic: 46.4 us -> 2.13 us
  matrix products: 36.7 us -> 0 us
    ppermute x5 -> x1, waiting for transfers between devices: 255 us -> 0.01 us  [rims(): incoming = lax.ppermute(outgoing, 'tile', [(0, 1), (1, 0)])]
    gather x60 -> x0, local copies, waits for them, and re-layouts: 183 us -> none  [the longest x15 93.1 us: one_block(): lead_tile = jnp.take(window, first_local, axis=1).astype(jnp.float32)]
    pallas_call x0 -> x4, Pallas kernels: none -> 139 us  [the longest x1 84.4 us: spread(): pl.pallas_call(functools.partial(spread_kernel, groups, width), out_shape...]
    dot_general x32 -> x0, matrix products: 36.7 us -> none  [the longest x15 25.3 us: one_block(): jnp.einsum('cprx,xk->cprk', product, col_taps, preferred_element_type=jnp...]
    convert_element_type x15 -> x0, other arithmetic: 33.5 us -> none  [one_block(): other_tile = jnp.take(window, second_local, axis=1).astype(jnp.float32)]
    another operation x15 -> x2, other arithmetic: 7.9 us -> 0.91 us  [rims(): return jnp.stack(pieces)]
    unnamed x12 -> x15, local copies, waits for them, and re-layouts: 10.8 us -> 5.22 us
  transfers between devices with their start and end apart: 5 -> 1, of which waited for: 4 -> 0; matrix products, arithmetic and copies ran while one was open for 1% -> 1% of each run, Pallas kernels for 0% -> 0%
where the time goes in v1:
time: 150 us; the launch traced here: 148 us
  Pallas kernels  139 us (93%)
  local copies, waits for them, and re-layouts  5.3 us (4%)
  other arithmetic  2.13 us (1%)
    pallas_call x1, Pallas kernels, spread(): pl.pallas_call(functools.partial(spread_kernel, groups, width), out_shape...  84.4 us
    pallas_call x1, Pallas kernels, work_pairs(): pl.pallas_call(functools.partial(pairs_kernel, rows, width), grid=(TOTAL...  34.5 us
    pallas_call x1, Pallas kernels, collect(): pl.pallas_call(functools.partial(collect_kernel, groups), out_shape=jax.S...  13.4 us
    pallas_call x1, Pallas kernels, to_slots(): pl.pallas_call(functools.partial(slots_kernel, count), out_shape=jax.Shap...  6.46 us
    unnamed x15, local copies, waits for them, and re-layouts  5.22 us
  transfers between devices with their start and end apart: 1, of which 0 were waited for; matrix products, arithmetic and copies ran while one was open for 1% of the time, Pallas kernels for 0%

profile of v1, /device:TPU:0, one launch (start us, length us, event | category | flops | bytes accessed | tf_op | source)
XLA Modules:
  0.0 147.5 jit_solution(5088199117995070394)
XLA Ops:
  0.0 1.2 fusion
  1.2 0.5 collective-permute-start
  2.4 0.8 copy.8.pair_list
  3.2 0.1 pad.15.clone
  3.3 0.0 collective-permute-done
  3.3 0.2 maximum_bitcast_fusion
  3.5 0.7 pad_maximum_fusion.rim
  4.2 0.0 copy-start.4
  4.2 0.0 copy-start.5
  4.2 0.0 copy-start.6
  4.2 84.4 %spread.1.held = bf16[2,31,32,1152]{3,2,1,0:T(8,128)(2,1)} custom-call(bf16[2,4,32,4096]{3,2,1,0:T(8,128)(2,1)} %acq.1, bf16[4,2,4,32,128]{4,3,2,1,0:T(8,128)(2,1)} %pad_maximum_fusion.rim), custom_call_target="tpu_custom_call" | custom-call | tf_op jit(solution)/shard_map/spread/pallas_call | solution.py:192
  88.6 0.0 copy-done.4
  88.6 0.0 copy-done.5
  88.6 0.0 copy-done.6
  88.6 0.0 copy-start
  88.6 2.3 %copy-done = bf16[2,31,32,1152]{3,2,1,0:T(8,128)(2,1)S(1)} copy-done((bf16[2,31,32,1152]{3,2,1,0:T(8,128)(2,1)S(1)}, bf16[2,31,32,1152]{3,2,1,0:T(8,128)(2,1)}, u32[]{:S(2)}) %copy-start) | copy-done | bytes 4571160
  90.9 0.0 copy-start.3
  90.9 34.5 %work_pairs.1.result = f32[240,8,128]{2,1,0:T(8,128)S(1)} custom-call(s32[240]{0:T(256)S(1)} %copy-done.5, s32[240]{0:T(256)S(1)} %copy-done.4, s32[8]{0:T(128)S(1)} %copy-done.6, s32[1]{0:T(128)S(6)} %copy.9.win_cols, bf16[2,31,32,1152]{3,2,1,0:T(8,128)(2,1)S(1)} %copy-done), custom_call_target="tpu_custom_call" | custom-call | tf_op jit(solution)/shard_map/work_pairs/pallas_call | solution.py:294
  125.4 0.0 copy-start.2
  125.4 0.9 copy-done.2
  126.4 13.4 %collect.1.parts = f32[4,60,8,128]{3,2,1,0:T(8,128)} custom-call(f32[240,8,128]{2,1,0:T(8,128)} %copy-done.2), custom_call_target="tpu_custom_call" | custom-call | tf_op jit(solution)/shard_map/collect/pallas_call | solution.py:414
  139.8 0.0 copy-done.3
  139.8 0.0 copy-start.1
  139.8 1.2 copy-done.1
  141.0 6.5 %to_slots.1 = f32[2,60,8,256]{3,2,1,0:T(8,128)} custom-call(s32[60,2]{1,0:T(8,128)S(1)} %copy.8.pair_list, s32[4,60]{1,0:T(4,128)S(1)} %copy-done.3, f32[4,60,8,128]{3,2,1,0:T(8,128)S(1)} %copy-done.1), custom_call_target="tpu_custom_call" | custom-call | tf_op jit(solution)/shard_map/to_slots/pallas_call | solution.py:453
  (2 shorter events, 0.0 us)
Async XLA Ops:
  1.2 2.0 %collective-permute-start = (bf16[2,4,32,8]{3,2,1,0:T(8,128)(2,1)S(1)}, bf16[2,4,32,8]{3,2,1,0:T(8,128)(2,1)S(1)}, u32[]{:S(2)}, u32[]{:S(2)}) collective-permute-start(bf16[2,4,32,8]{3,2,1,0:T(8,128)(2,1)S(1)} %get-tuple-element.9), channel_id=1, source_target_pairs={{0,1},{1,0},{2,3},{3,2},{4,5},{5,4},{6,7},{7,6},{8,9},{9,8},{10,11... | collective-permute-start | bytes 12296 | tf_op jit(solution)/shard_map/ppermute | solution.py:470
  4.2 84.4 %copy-start.4 = (s32[240]{0:T(256)S(1)}, s32[240]{0:T(256)}, u32[]{:S(2)}) copy-start(s32[240]{0:T(256)} %constant.18.clone.second) | copy-start | bytes 2884
  4.2 84.4 %copy-start.5 = (s32[240]{0:T(256)S(1)}, s32[240]{0:T(256)}, u32[]{:S(2)}) copy-start(s32[240]{0:T(256)} %constant.6.clone.first) | copy-start | bytes 2884
  4.2 84.4 %copy-start.6 = (s32[8]{0:T(128)S(1)}, s32[8]{0:T(128)}, u32[]{:S(2)}) copy-start(s32[8]{0:T(128)} %win_rows.1) | copy-start | bytes 100
  88.6 2.3 %copy-start = (bf16[2,31,32,1152]{3,2,1,0:T(8,128)(2,1)S(1)}, bf16[2,31,32,1152]{3,2,1,0:T(8,128)(2,1)}, u32[]{:S(2)}) copy-start(bf16[2,31,32,1152]{3,2,1,0:T(8,128)(2,1)} %spread.1.held) | copy-start | bytes 13713412
  90.9 48.9 %copy-start.3 = (s32[4,60]{1,0:T(4,128)S(1)}, s32[4,60]{1,0:T(4,128)}, u32[]{:S(2)}) copy-start(s32[4,60]{1,0:T(4,128)} %constant.19.clone.place) | copy-start | bytes 2884
  125.4 0.9 copy-start.2
  139.8 1.2 copy-start.1

commit v2 on v1

--- a/solution.py
+++ b/solution.py
@@ -125,8 +125,6 @@
         pltpu.make_async_copy(body_of(member), main, local.at[0]),
         pltpu.make_async_copy(rim_of(member), side, local.at[1]),
     ]
-    for copy in mine:
-        copy.start()
 
     onward = [
         (0, OWN, LOCAL, -1),
@@ -137,14 +135,33 @@
 
     def far(source):
         start, count, place, step = onward[source]
-        return pltpu.make_async_remote_copy(
-            src_ref=held.at[:, pl.ds(start, count)],
-            dst_ref=held.at[:, pl.ds(place, count)],
-            send_sem=far_send.at[source],
-            recv_sem=far_recv.at[source],
-            device_id={"date": date + step * GROUP},
-            device_id_type=MESH,
-        )
+        return [
+            pltpu.make_async_remote_copy(
+                src_ref=src,
+                dst_ref=dst,
+                send_sem=far_send.at[source, n],
+                recv_sem=far_recv.at[source, n],
+                device_id={"date": date + step * GROUP},
+                device_id_type=MESH,
+            )
+            for n, (src, dst) in enumerate(zip(slot(start, count), slot(place, count)))
+        ]
+
+    def far_mine(source):
+        start, count, place, step = onward[source]
+        skip = start - source * OWN
+        main, side = slot(place, count)
+        return [
+            pltpu.make_async_remote_copy(
+                src_ref=src.at[:, pl.ds(skip, count)],
+                dst_ref=dst,
+                send_sem=far_send.at[source, n],
+                recv_sem=far_recv.at[source, n],
+                device_id={"date": date + step * GROUP},
+                device_id_type=MESH,
+            )
+            for n, (src, dst) in enumerate(((body_of(source), main), (rim_of(source), side)))
+        ]
 
     def pass_on(who):
         for source in range(GROUP):
@@ -152,15 +169,25 @@
 
             @pl.when(jnp.logical_and(who == source, exists))
             def _():
-                far(source).start()
+                for copy in far(source):
+                    copy.start()
+
+    for source in range(GROUP):
+        exists = has_before if onward[source][3] < 0 else has_after
+
+        @pl.when(jnp.logical_and(member == source, exists))
+        def _():
+            for copy in far_mine(source):
+                copy.start()
 
     for copy in mine:
-        copy.wait()
-    pass_on(member)
+        copy.start()
     for k in (1, 2, 3):
         for copy in near[k - 1]:
             copy.wait_recv()
         pass_on(other_member(member, k))
+    for copy in mine:
+        copy.wait()
     for pair in near:
         for copy in pair:
             copy.wait_send()
@@ -172,19 +199,13 @@
 
         @pl.when(sends)
         def _():
-            far(source).wait_send()
+            for copy in far(source):
+                copy.wait_send()
 
         @pl.when(gets)
         def _():
-            far(source).wait_recv()
-
-        @pl.when(jnp.logical_not(gets))
-        def _():
-            fill = pltpu.make_async_copy(
-                held.at[:, pl.ds(start, count)], held.at[:, pl.ds(place, count)], local.at[2]
-            )
-            fill.start()
-            fill.wait()
+            for copy in far(source):
+                copy.wait_recv()
 
 
 def spread(acq, rim, groups):
@@ -197,9 +218,9 @@
         scratch_shapes=[
             pltpu.SemaphoreType.DMA((GROUP, 2)),
             pltpu.SemaphoreType.DMA((GROUP, 2)),
-            pltpu.SemaphoreType.DMA((GROUP,)),
-            pltpu.SemaphoreType.DMA((GROUP,)),
-            pltpu.SemaphoreType.DMA((3,)),
+            pltpu.SemaphoreType.DMA((GROUP, 2)),
+            pltpu.SemaphoreType.DMA((GROUP, 2)),
+            pltpu.SemaphoreType.DMA((2,)),
         ],
         compiler_params=pltpu.CompilerParams(collective_id=0, has_side_effects=True),
         name="spread",
@@ -215,13 +236,34 @@
 
 
 def pairs_kernel(
-    rows, width, first, second, win_rows, win_cols, held, result, product, col_taps, row_taps, power
+    rows,
+    width,
+    groups,
+    first,
+    second,
+    win_rows,
+    win_cols,
+    held,
+    result,
+    wide,
+    product,
+    col_taps,
+    row_taps,
+    power,
 ):
     out_rows = rows // STRIDE_R
     out_cols = width // STRIDE_C
     full = width + LANES
     step = pl.program_id(0)
     cuts = [(r, c) for r in range(0, rows, 16) for c in range(0, full, 384)]
+    group = lax.axis_index("date") // GROUP
+
+    def present(d):
+        missing = jnp.logical_or(
+            jnp.logical_and(group == 0, d >= LOCAL + DOWN),
+            jnp.logical_and(group == groups - 1, jnp.logical_and(d >= LOCAL, d < LOCAL + DOWN)),
+        )
+        return jnp.where(missing, 0, d)
 
     @pl.when(step == 0)
     def _():
@@ -246,8 +288,10 @@
 
         def one_date(d, carry):
             for r, c in cuts:
-                re = held[0, d, r : r + 16, c : c + 384].astype(jnp.float32)
-                im = held[1, d, r : r + 16, c : c + 384].astype(jnp.float32)
+                re = held[0, present(d), r : r + 16, c : c + 384].astype(jnp.float32)
+                im = held[1, present(d), r : r + 16, c : c + 384].astype(jnp.float32)
+                wide[0, d, r : r + 16, c : c + 384] = re
+                wide[1, d, r : r + 16, c : c + 384] = im
                 at = pl.multiple_of(d * rows + r, 16)
                 product[pl.ds(at, 16), c : c + 384] = (re * re + im * im).astype(jnp.bfloat16)
             return carry
@@ -264,10 +308,10 @@
         i = first[step * CHUNK + p]
         j = second[step * CHUNK + p]
         for r, c in cuts:
-            re_i = held[0, i, r : r + 16, c : c + 384].astype(jnp.float32)
-            im_i = held[1, i, r : r + 16, c : c + 384].astype(jnp.float32)
-            re_j = held[0, j, r : r + 16, c : c + 384].astype(jnp.float32)
-            im_j = held[1, j, r : r + 16, c : c + 384].astype(jnp.float32)
+            re_i = wide[0, i, r : r + 16, c : c + 384]
+            im_i = wide[1, i, r : r + 16, c : c + 384]
+            re_j = wide[0, j, r : r + 16, c : c + 384]
+            im_j = wide[1, j, r : r + 16, c : c + 384]
             at = pl.multiple_of(p * 2 * rows + r, 16)
             product[pl.ds(at, 16), c : c + 384] = (re_i * re_j + im_i * im_j).astype(jnp.bfloat16)
             at = pl.multiple_of(p * 2 * rows + rows + r, 16)
@@ -286,18 +330,19 @@
         result[p] = looked[p] * lax.rsqrt(power[i] * power[j] + EPS)
 
 
-def work_pairs(held, win_rows, win_cols):
+def work_pairs(held, win_rows, win_cols, groups):
     rows, full = held.shape[2:]
     width = full - LANES
     out_rows = rows // STRIDE_R
     smem = pl.BlockSpec(memory_space=pltpu.SMEM)
     return pl.pallas_call(
-        functools.partial(pairs_kernel, rows, width),
+        functools.partial(pairs_kernel, rows, width, groups),
         grid=(TOTAL // CHUNK,),
         out_shape=jax.ShapeDtypeStruct((TOTAL, out_rows, LANES), jnp.float32),
         in_specs=[smem, smem, smem, smem, pl.BlockSpec(held.shape, lambda s: (0, 0, 0, 0))],
         out_specs=pl.BlockSpec((CHUNK, out_rows, LANES), lambda s: (s, 0, 0)),
         scratch_shapes=[
+            pltpu.VMEM(held.shape, jnp.float32),
             pltpu.VMEM((2 * CHUNK * rows, full), jnp.bfloat16),
             pltpu.VMEM((full, LANES), jnp.bfloat16),
             pltpu.VMEM((CHUNK * out_rows, CHUNK * rows), jnp.bfloat16),
@@ -482,7 +527,7 @@
 
 def shards(groups, acquisitions, pair_list, win_rows, win_cols):
     held = spread(acquisitions, rims(acquisitions), groups)
-    result = work_pairs(held, win_rows, win_cols)
+    result = work_pairs(held, win_rows, win_cols, groups)
     parts = collect(result, groups)
     return to_slots(pair_list, parts)
 

time: 150 us -> 107 us (0.71); the launches traced: 148 us -> 107 us
  Pallas kernels: 139 us -> 98 us
    pallas_call x1, Pallas kernels: 84.4 us -> 45.1 us  [spread(): pl.pallas_call(functools.partial(spread_kernel, groups, width), out_shape...]
    pallas_call x1, Pallas kernels: 34.5 us -> 30.8 us  [work_pairs(): pl.pallas_call(functools.partial(pairs_kernel, rows, width, groups), grid...]
    pallas_call x1, Pallas kernels: 13.4 us -> 15.7 us  [collect(): pl.pallas_call(functools.partial(collect_kernel, groups), out_shape=jax.S...]
where the time goes in v2:
time: 107 us
  Pallas kernels  98 us (92%)
  local copies, waits for them, and re-layouts  5.3 us (5%)
  other arithmetic  2.13 us (2%)
    pallas_call x1, Pallas kernels, spread(): pl.pallas_call(functools.partial(spread_kernel, groups, width), out_shape...  45.1 us
    pallas_call x1, Pallas kernels, work_pairs(): pl.pallas_call(functools.partial(pairs_kernel, rows, width, groups), grid...  30.8 us
    pallas_call x1, Pallas kernels, collect(): pl.pallas_call(functools.partial(collect_kernel, groups), out_shape=jax.S...  15.7 us
    pallas_call x1, Pallas kernels, to_slots(): pl.pallas_call(functools.partial(slots_kernel, count), out_shape=jax.Shap...  6.46 us
    unnamed x15, local copies, waits for them, and re-layouts  5.22 us
  transfers between devices with their start and end apart: 1, of which 0 were waited for; matrix products, arithmetic and copies ran while one was open for 1% of the time, Pallas kernels for 0%

profile of v2, /device:TPU:0, one launch (start us, length us, event | category | flops | bytes accessed | tf_op | source)
XLA Modules:
  0.0 106.7 jit_solution(14543133239225665648)
XLA Ops:
  0.0 1.2 %fusion = (bf16[2,4,32,8]{3,2,1,0:T(8,128)(2,1)S(1)}, bf16[2,4,32,8]{3,2,1,0:T(8,128)(2,1)S(1)}, bf16[2,4,32,8]{3,2,1,0:T(8,128)(2,1)S(1)}, bf16[2,4,32,8]{3,2,1...) fusion(bf16[2,4,32,4096]{3,2,1,0:T(8,128)(2,1)} %acq.1, ...), kind=kLoop, calls=%fused_computation.8 | loop fusion | flops 2048 | bytes 61441 | tf_op jit(solution)/shard_map/slice | solution.py:523
  1.2 0.5 collective-permute-start
  2.4 0.8 copy.8.pair_list
  3.2 0.1 pad.15.clone
  3.3 0.0 collective-permute-done
  3.3 0.2 maximum_bitcast_fusion
  3.5 0.7 pad_maximum_fusion.rim
  4.2 0.0 copy-start.4
  4.2 0.0 copy-start.5
  4.2 0.0 copy-start.6
  4.2 45.1 %spread.1.held = bf16[2,31,32,1152]{3,2,1,0:T(8,128)(2,1)} custom-call(bf16[2,4,32,4096]{3,2,1,0:T(8,128)(2,1)} %acq.1, bf16[4,2,4,32,128]{4,3,2,1,0:T(8,128)(2,1)} %pad_maximum_fusion.rim), custom_call_target="tpu_custom_call" | custom-call | tf_op jit(solution)/shard_map/spread/pallas_call | solution.py:213
  49.3 0.0 copy-done.4
  49.3 0.0 copy-done.5
  49.3 0.0 copy-done.6
  49.3 0.0 copy-start
  49.3 2.3 %copy-done = bf16[2,31,32,1152]{3,2,1,0:T(8,128)(2,1)S(1)} copy-done((bf16[2,31,32,1152]{3,2,1,0:T(8,128)(2,1)S(1)}, bf16[2,31,32,1152]{3,2,1,0:T(8,128)(2,1)}, u32[]{:S(2)}) %copy-start) | copy-done | bytes 4571160
  51.6 0.0 copy-start.3
  51.6 30.8 %work_pairs.1.result = f32[240,8,128]{2,1,0:T(8,128)S(1)} custom-call(s32[240]{0:T(256)S(1)} %copy-done.5, s32[240]{0:T(256)S(1)} %copy-done.4, s32[8]{0:T(128)S(1)} %copy-done.6, s32[1]{0:T(128)S(6)} %copy.9.win_cols, bf16[2,31,32,1152]{3,2,1,0:T(8,128)(2,1)S(1)} %copy-done), custom_call_target="tpu_custom_call" | custom-call | tf_op jit(solution)/shard_map/work_pairs/pallas_call | solution.py:338
  82.4 0.0 copy-start.2
  82.4 0.9 copy-done.2
  83.3 15.7 %collect.1.parts = f32[4,60,8,128]{3,2,1,0:T(8,128)} custom-call(f32[240,8,128]{2,1,0:T(8,128)} %copy-done.2), custom_call_target="tpu_custom_call" | custom-call | tf_op jit(solution)/shard_map/collect/pallas_call | solution.py:459
  99.0 0.0 copy-done.3
  99.0 0.0 copy-start.1
  99.1 1.2 %copy-done.1 = f32[4,60,8,128]{3,2,1,0:T(8,128)S(1)} copy-done((f32[4,60,8,128]{3,2,1,0:T(8,128)S(1)}, f32[4,60,8,128]{3,2,1,0:T(8,128)}, u32[]{:S(2)}) %copy-start.1) | copy-done | bytes 983064
  100.2 6.5 %to_slots.1 = f32[2,60,8,256]{3,2,1,0:T(8,128)} custom-call(s32[60,2]{1,0:T(8,128)S(1)} %copy.8.pair_list, s32[4,60]{1,0:T(4,128)S(1)} %copy-done.3, f32[4,60,8,128]{3,2,1,0:T(8,128)S(1)} %copy-done.1), custom_call_target="tpu_custom_call" | custom-call | tf_op jit(solution)/shard_map/to_slots/pallas_call | solution.py:498
  (2 shorter events, 0.0 us)
Async XLA Ops:
  1.2 2.0 %collective-permute-start = (bf16[2,4,32,8]{3,2,1,0:T(8,128)(2,1)S(1)}, bf16[2,4,32,8]{3,2,1,0:T(8,128)(2,1)S(1)}, u32[]{:S(2)}, u32[]{:S(2)}) collective-permute-start(bf16[2,4,32,8]{3,2,1,0:T(8,128)(2,1)S(1)} %get-tuple-element.9), channel_id=1, source_target_pairs={{0,1},{1,0},{2,3},{3,2},{4,5},{5,4},{6,7},{7,6},{8,9},{9,8},{10,11... | collective-permute-start | bytes 12296 | tf_op jit(solution)/shard_map/ppermute | solution.py:515
  4.2 45.1 %copy-start.4 = (s32[240]{0:T(256)S(1)}, s32[240]{0:T(256)}, u32[]{:S(2)}) copy-start(s32[240]{0:T(256)} %constant.18.clone.second) | copy-start | bytes 2884
  4.2 45.1 %copy-start.5 = (s32[240]{0:T(256)S(1)}, s32[240]{0:T(256)}, u32[]{:S(2)}) copy-start(s32[240]{0:T(256)} %constant.6.clone.first) | copy-start | bytes 2884
  4.2 45.1 %copy-start.6 = (s32[8]{0:T(128)S(1)}, s32[8]{0:T(128)}, u32[]{:S(2)}) copy-start(s32[8]{0:T(128)} %win_rows.1) | copy-start | bytes 100
  49.3 2.3 %copy-start = (bf16[2,31,32,1152]{3,2,1,0:T(8,128)(2,1)S(1)}, bf16[2,31,32,1152]{3,2,1,0:T(8,128)(2,1)}, u32[]{:S(2)}) copy-start(bf16[2,31,32,1152]{3,2,1,0:T(8,128)(2,1)} %spread.1.held) | copy-start | bytes 13713412
  51.6 47.4 %copy-start.3 = (s32[4,60]{1,0:T(4,128)S(1)}, s32[4,60]{1,0:T(4,128)}, u32[]{:S(2)}) copy-start(s32[4,60]{1,0:T(4,128)} %constant.19.clone.place) | copy-start | bytes 2884
  82.4 0.9 copy-start.2
  99.0 1.2 %copy-start.1 = (f32[4,60,8,128]{3,2,1,0:T(8,128)S(1)}, f32[4,60,8,128]{3,2,1,0:T(8,128)}, u32[]{:S(2)}) copy-start(f32[4,60,8,128]{3,2,1,0:T(8,128)} %collect.1.parts) | copy-start | bytes 2949124

commit v3 on v0

v3 whole, which is shorter than its diff:
```python
import functools

import jax
import jax.numpy as jnp
from jax import lax
from jax.experimental import pallas as pl
from jax.experimental.pallas import tpu as pltpu
from jax.sharding import PartitionSpec as P

SPAN = 15
STRIDE_R = 4
STRIDE_C = 16
EPS = 1e-06

GROUP = 4
OWN = 4
LOCAL = GROUP * OWN
DOWN = 8
UP_FROM = DOWN + 1
UP = LOCAL - UP_FROM
HELD = LOCAL + DOWN + UP
HALF = STRIDE_C // 2
LANES = 128
CHUNK = 24
MESH = pl.DeviceIdType.MESH


INSIDE = LOCAL * (LOCAL - 1) // 2
RECT = (LOCAL - DOWN) * DOWN
FOLD = DOWN * (DOWN - 1) // 2
UPS = (0, 0, 6, 22)
OUTBOX = LOCAL * SPAN


def other_member(member, k):
    if k == 1:
        return member + 1 - 2 * (member % 2)
    if k == 2:
        return member + 2 - 4 * (member // 2)
    return GROUP - 1 - member


def inside_pair(f):
    x = lax.rem(f, LOCAL)
    y = x + lax.div(f, LOCAL) + 1
    turn = lax.div(y, LOCAL)
    i = x * (1 - turn) + (y - LOCAL) * turn
    j = y * (1 - turn) + x * turn
    return i, j, i * SPAN + j - i - 1


def cross_pair(f):
    beyond = lax.div(f, RECT)
    up = lax.div(f, RECT + FOLD)
    e = (f - RECT - FOLD * up) * beyond
    row = lax.div(e, DOWN - 1)
    col = lax.rem(e, DOWN - 1)
    turn = lax.div(col + row, DOWN - 1)
    size = (DOWN - 1 - row) * (1 - turn) + row * turn
    inner = col - (DOWN - 1 - row) * turn
    i = (1 - beyond) * (DOWN + lax.div(f, DOWN)) + (beyond - up) * size
    j = (1 - beyond) * lax.rem(f, DOWN) + (beyond - up) * inner + LOCAL
    i = (1 - up) * i + up * (LOCAL + DOWN + size - 1)
    j = (1 - up) * j + up * (DOWN + inner)
    near = i * SPAN + j - i - 1
    far = OUTBOX + lax.div(size * (size - 1), 2) + inner
    return i, j, (1 - up) * near + up * far


def split_dot(taps, values):
    high = values.astype(jnp.bfloat16)
    low = (values - high.astype(jnp.float32)).astype(jnp.bfloat16)
    return jnp.dot(taps, high, preferred_element_type=jnp.float32) + jnp.dot(
        taps, low, preferred_element_type=jnp.float32
    )


def strip_kernel(
    groups,
    rows,
    width,
    win_rows,
    win_cols,
    acq,
    rim,
    parts,
    held,
    wide,
    product,
    col_taps,
    row_taps,
    power,
    looked,
    outbox,
    send,
    recv,
    far_send,
    far_recv,
    local,
    back_send,
    back_recv,
    up_send,
    up_recv,
):
    out_rows = rows // STRIDE_R
    out_cols = width // STRIDE_C
    full = width + LANES
    cuts = [(r, c) for r in range(0, rows, 16) for c in range(0, full, 384)]
    date = lax.axis_index("date")
    group, member = date // GROUP, date % GROUP
    base = group * GROUP
    has_before, has_after = group > 0, group < groups - 1
    is_late = member >= 2

    def greet(where):
        pl.semaphore_signal(
            pltpu.get_barrier_semaphore(),
            inc=1,
            device_id={"date": where},
            device_id_type=MESH,
        )

    for k in (1, 2, 3):
        greet(base + other_member(member, k))

    @pl.when(has_before)
    def _():
        greet(date - GROUP)
        for k in (2, 3):

            @pl.when(member != k)
            def _():
                greet(base - GROUP + k)

    @pl.when(has_after)
    def _():
        greet(date + GROUP)

        @pl.when(is_late)
        def _():
            for k in (1, 2, 3):
                greet(base + GROUP + other_member(member, k))

    late = member // 2
    peers = GROUP - 1 + has_before.astype(jnp.int32) * (3 - late)
    peers = peers + has_after.astype(jnp.int32) * (1 + 3 * late)
    pl.semaphore_wait(pltpu.get_barrier_semaphore(), peers)

    def body_of(who):
        return acq.at[:, :, :, pl.ds(pl.multiple_of(who * width, width), width)]

    def rim_of(who):
        return rim.at[who]

    def slot(start, count):
        part = held.at[:, pl.ds(start, count)]
        return part.at[:, :, :, pl.ds(0, width)], part.at[:, :, :, pl.ds(width, LANES)]

    def remote(src, dst, send_sem, recv_sem, where):
        return pltpu.make_async_remote_copy(
            src_ref=src,
            dst_ref=dst,
            send_sem=send_sem,
            recv_sem=recv_sem,
            device_id={"date": where},
            device_id_type=MESH,
        )

    onward = [
        (0, OWN, LOCAL, -1),
        (OWN, OWN, LOCAL + OWN, -1),
        (UP_FROM, 3 * OWN - UP_FROM, LOCAL + DOWN, 1),
        (3 * OWN, OWN, LOCAL + DOWN + 3 * OWN - UP_FROM, 1),
    ]

    def far(source, mine):
        start, count, place, step = onward[source]
        if mine:
            skip = start - source * OWN
            srcs = [ref.at[:, pl.ds(skip, count)] for ref in (body_of(source), rim_of(source))]
        else:
            srcs = slot(start, count)
        return [
            remote(
                src, dst, far_send.at[source, n], far_recv.at[source, n], date + step * GROUP
            )
            for n, (src, dst) in enumerate(zip(srcs, slot(place, count)))
        ]

    def pass_on(who, mine):
        for source in range(GROUP):
            exists = has_before if onward[source][3] < 0 else has_after

            @pl.when(jnp.logical_and(who == source, exists))
            def _():
                for copy in far(source, mine):
                    copy.start()

    near = []
    for k in (1, 2, 3):
        who = other_member(member, k)
        pair = [
            remote(src, dst, send.at[k, n], recv.at[k, n], base + who)
            for n, (src, dst) in enumerate(
                zip((body_of(who), rim_of(who)), slot(member * OWN, OWN))
            )
        ]
        for copy in pair:
            copy.start()
        near.append(pair)
    pass_on(member, True)
    main, side = slot(member * OWN, OWN)
    mine = [
        pltpu.make_async_copy(body_of(member), main, local.at[0]),
        pltpu.make_async_copy(rim_of(member), side, local.at[1]),
    ]
    for copy in mine:
        copy.start()

    lane = lax.broadcasted_iota(jnp.int32, (full, LANES), 0)
    out = lax.broadcasted_iota(jnp.int32, (full, LANES), 1) % out_cols
    column = jnp.where(
        lane < width, lane, jnp.where(lane < width + HALF, lane - width - HALF, lane - HALF)
    )
    beside = jnp.abs(2 * column + 1 - (2 * out + 1) * STRIDE_C) <= win_cols[0]
    beside = jnp.logical_and(beside, lane < width + 2 * HALF)
    col_taps[...] = jnp.where(beside, 1.0, 0.0).astype(jnp.bfloat16)
    shape = (CHUNK * out_rows, CHUNK * rows)
    at = lax.broadcasted_iota(jnp.int32, shape, 0)
    row = lax.broadcasted_iota(jnp.int32, shape, 1)
    window = jnp.zeros(shape, jnp.int32)
    for o in range(out_rows):
        window = jnp.where(at % out_rows == o, win_rows[o], window)
    inside = jnp.abs(2 * (row % rows) + 1 - (2 * (at % out_rows) + 1) * STRIDE_R) <= window
    inside = jnp.logical_and(inside, at // out_rows == row // rows)
    row_taps[...] = jnp.where(inside, 1.0, 0.0).astype(jnp.bfloat16)

    def widen(start, count, shift):
        def one_date(n, carry):
            d = start + n
            for r, c in cuts:
                re = held[0, d, r : r + 16, c : c + 384].astype(jnp.float32)
                im = held[1, d, r : r + 16, c : c + 384].astype(jnp.float32)
                wide[0, d, r : r + 16, c : c + 384] = re
                wide[1, d, r : r + 16, c : c + 384] = im
                to = pl.multiple_of((d - shift) * rows + r, 16)
                product[pl.ds(to, 16), c : c + 384] = (re * re + im * im).astype(jnp.bfloat16)
            return carry

        lax.fori_loop(0, count, one_date, 0)

    def blank(start, count, shift):
        def one_date(n, carry):
            d = start + n
            for part in range(2):
                wide[part, d] = jnp.zeros((rows, full), jnp.float32)
            to = pl.multiple_of((d - shift) * rows, 16)
            product[pl.ds(to, rows), :] = jnp.zeros((rows, full), jnp.bfloat16)
            return carry

        lax.fori_loop(0, count, one_date, 0)

    def look_power(start):
        across = jnp.dot(
            product[: LOCAL * rows], col_taps[...], preferred_element_type=jnp.float32
        )
        taps = row_taps[: LOCAL * out_rows, : LOCAL * rows]
        power[start : start + LOCAL] = split_dot(taps, across).reshape(LOCAL, out_rows, LANES)

    def work(total, pair_of):
        def one_chunk(chunk, carry):
            def one_pair(p, carry):
                i, j, _ = pair_of(chunk * CHUNK + p)
                for r, c in cuts:
                    re_i = wide[0, i, r : r + 16, c : c + 384]
                    im_i = wide[1, i, r : r + 16, c : c + 384]
                    re_j = wide[0, j, r : r + 16, c : c + 384]
                    im_j = wide[1, j, r : r + 16, c : c + 384]
                    re = (re_i * re_j + im_i * im_j).astype(jnp.bfloat16)
                    im = (im_i * re_j - re_i * im_j).astype(jnp.bfloat16)
                    product[pl.ds(pl.multiple_of(p * 2 * rows + r, 16), 16), c : c + 384] = re
                    at = pl.multiple_of(p * 2 * rows + rows + r, 16)
                    product[pl.ds(at, 16), c : c + 384] = im
                return carry

            lax.fori_loop(0, CHUNK, one_pair, 0)
            across = jnp.dot(product[...], col_taps[...], preferred_element_type=jnp.float32)
            across = across.reshape(CHUNK, 2, rows, LANES)
            left = lax.broadcasted_iota(jnp.int32, (CHUNK, rows, LANES), 2) < out_cols
            both = jnp.where(left, across[:, 0], across[:, 1]).reshape(CHUNK * rows, LANES)
            looked[...] = split_dot(row_taps[...], both).reshape(CHUNK, out_rows, LANES)

            def finish(p, carry):
                i, j, to = pair_of(chunk * CHUNK + p)
                outbox[to] = looked[p] * lax.rsqrt(power[i] * power[j] + EPS)
                return carry

            lax.fori_loop(0, CHUNK, finish, 0)
            return carry

        lax.fori_loop(0, total // CHUNK, one_chunk, 0)

    def back(source, target, step, part):
        i = target * OWN + step
        if part == 0:
            start, count = 0, SPAN - i
        else:
            start, count = SPAN - i, min(i, DOWN)
        src = outbox.at[pl.ds(i * SPAN + start, count)]
        dst = parts.at[source, pl.ds(step * SPAN + start, count)]
        return src, dst, count

    def back_copies(source, target, part):
        copies = []
        for step in range(OWN):
            src, dst, count = back(source, target, step, part)
            if count:
                copies.append(
                    remote(
                        src,
                        dst,
                        back_send.at[part, target, step],
                        back_recv.at[part, source, step],
                        base + target,
                    )
                )
        return copies

    def kept_copies(target, part):
        copies = []
        for step in range(OWN):
            src, dst, count = back(target, target, step, part)
            if count:
                sem = back_send.at[part, target, step]
                copies.append(pltpu.make_async_copy(src, dst, sem))
        return copies

    def give_back(part):
        for target in range(GROUP):

            @pl.when(member != target)
            def _():
                for copy in back_copies(member, target, part):
                    copy.start()

            @pl.when(member == target)
            def _():
                for copy in kept_copies(target, part):
                    copy.start()

    def end_back(part):
        for target in range(GROUP):

            @pl.when(member != target)
            def _():
                for copy in back_copies(member, target, part):
                    copy.wait_send()

            @pl.when(member == target)
            def _():
                for copy in kept_copies(target, part):
                    copy.wait()
                for source in range(GROUP):
                    if source != target:
                        for copy in back_copies(source, target, part):
                            copy.wait_recv()

    def up_copy(source, target):
        start = OUTBOX + sum(UPS[:target])
        return remote(
            outbox.at[pl.ds(start, UPS[target])],
            parts.at[source, pl.ds(OWN * SPAN, UPS[target])],
            up_send.at[target],
            up_recv.at[source],
            base - GROUP + target,
        )

    for copy in mine:
        copy.wait()
    widen(member * OWN, OWN, 0)
    for k in (1, 2, 3):
        for copy in near[k - 1]:
            copy.wait_recv()
        who = other_member(member, k)
        pass_on(who, False)
        widen(who * OWN, OWN, 0)
    look_power(0)
    work(INSIDE, inside_pair)
    give_back(0)

    for source in range(GROUP):
        start, count, place, step = onward[source]
        gets = has_after if step < 0 else has_before

        @pl.when(gets)
        def _():
            for copy in far(source, False):
                copy.wait_recv()
            widen(place, count, LOCAL)

        @pl.when(jnp.logical_not(gets))
        def _():
            blank(place, count, LOCAL)

    look_power(LOCAL)
    work(RECT + 2 * FOLD, cross_pair)
    give_back(1)

    @pl.when(has_before)
    def _():
        for target in (2, 3):
            up_copy(member, target).start()

    for pair in near:
        for copy in pair:
            copy.wait_send()
    for source in range(GROUP):
        exists = has_before if onward[source][3] < 0 else has_after

        @pl.when(exists)
        def _():
            for copy in far(source, False):
                copy.wait_send()

    end_back(0)
    end_back(1)

    @pl.when(has_before)
    def _():
        for target in (2, 3):
            up_copy(member, target).wait_send()

    for target in (2, 3):

        @pl.when(jnp.logical_and(has_after, member == target))
        def _():
            for source in range(GROUP):
                up_copy(source, target).wait_recv()


def strip(acq, rim, win_rows, win_cols, groups):
    rows = acq.shape[2]
    width = acq.shape[3] // GROUP
    full = width + LANES
    out_rows = rows // STRIDE_R
    dates = (2, HELD, rows, full)
    smem = pl.BlockSpec(memory_space=pltpu.SMEM)
    hbm = pl.BlockSpec(memory_space=pl.ANY)
    dma = pltpu.SemaphoreType.DMA
    return pl.pallas_call(
        functools.partial(strip_kernel, groups, rows, width),
        out_shape=jax.ShapeDtypeStruct(
            (GROUP, OWN * SPAN + max(UPS), out_rows, LANES), jnp.float32
        ),
        in_specs=[smem, smem, hbm, hbm],
        out_specs=hbm,
        scratch_shapes=[
            pltpu.VMEM(dates, acq.dtype),
            pltpu.VMEM(dates, jnp.float32),
            pltpu.VMEM((2 * CHUNK * rows, full), jnp.bfloat16),
            pltpu.VMEM((full, LANES), jnp.bfloat16),
            pltpu.VMEM((CHUNK * out_rows, CHUNK * rows), jnp.bfloat16),
            pltpu.VMEM((2 * LOCAL, out_rows, LANES), jnp.float32),
            pltpu.VMEM((CHUNK, out_rows, LANES), jnp.float32),
            pltpu.VMEM((OUTBOX + FOLD, out_rows, LANES), jnp.float32),
            dma((GROUP, 2)),
            dma((GROUP, 2)),
            dma((GROUP, 2)),
            dma((GROUP, 2)),
            dma((2,)),
            dma((2, GROUP, OWN)),
            dma((2, GROUP, OWN)),
            dma((GROUP,)),
            dma((GROUP,)),
        ],
        compiler_params=pltpu.CompilerParams(
            collective_id=0, has_side_effects=True, vmem_limit_bytes=48 * 2**20
        ),
        name="strip",
    )(win_rows, win_cols, acq, rim)


def slots_kernel(count, pair_list, parts, out):
    date = lax.axis_index("date")
    member = date % GROUP
    half = LANES // 2
    left = lax.broadcasted_iota(jnp.int32, (parts.shape[2], LANES), 1) < half

    def one_slot(s, carry):
        i = pair_list[s, 0]
        alive = i >= 0
        step = i - date * OWN
        far = pair_list[s, 1] - i - 1
        at = step * SPAN + far
        size = member * OWN + step - DOWN
        later = size + far - SPAN
        gone = jnp.logical_and(size > 0, jnp.logical_and(later >= 0, later < size))
        first_up = jnp.maximum(member * OWN - DOWN, 1)
        behind = (size * (size - 1) - first_up * (first_up - 1)) // 2 + later
        at = jnp.where(gone, OWN * SPAN + behind, at)
        at = jnp.clip(jnp.where(alive, at, 0), 0, parts.shape[1] - 1)
        for n in range(GROUP // 2):
            a = parts[2 * n, at]
            b = parts[2 * n + 1, at]
            re = jnp.where(left, a, pltpu.roll(b, half, 1))
            im = jnp.where(left, pltpu.roll(a, half, 1), b)
            out[0, s, :, n * LANES : (n + 1) * LANES] = jnp.where(alive, re, 0.0)
            out[1, s, :, n * LANES : (n + 1) * LANES] = jnp.where(alive, im, 0.0)
        return carry

    lax.fori_loop(0, count, one_slot, 0)


def to_slots(pair_list, parts):
    count = pair_list.shape[0]
    smem = pl.BlockSpec(memory_space=pltpu.SMEM)
    vmem = pl.BlockSpec(memory_space=pltpu.VMEM)
    return pl.pallas_call(
        functools.partial(slots_kernel, count),
        out_shape=jax.ShapeDtypeStruct(
            (2, count, parts.shape[2], GROUP * LANES // 2), jnp.float32
        ),
        in_specs=[smem, vmem],
        out_specs=vmem,
        compiler_params=pltpu.CompilerParams(vmem_limit_bytes=16 * 2**20),
        name="to_slots",
    )(pair_list, parts)


def rims(acq):
    cols = acq.shape[3]
    width = cols // GROUP
    tile = lax.axis_index("tile")
    outgoing = jnp.where(tile == 0, acq[..., cols - HALF :], acq[..., :HALF])
    incoming = lax.ppermute(outgoing, "tile", [(0, 1), (1, 0)])
    nothing = jnp.zeros_like(incoming)
    lower = jnp.where(tile == 1, incoming, nothing)
    upper = jnp.where(tile == 0, incoming, nothing)
    pad = jnp.zeros((*acq.shape[:3], LANES - 2 * HALF), acq.dtype)
    pieces = []
    for k in range(GROUP):
        left = lower if k == 0 else acq[..., k * width - HALF : k * width]
        right = upper if k == GROUP - 1 else acq[..., (k + 1) * width : (k + 1) * width + HALF]
        pieces.append(jnp.concatenate((left, right, pad), axis=3))
    return jnp.stack(pieces)


def shards(groups, acquisitions, pair_list, win_rows, win_cols):
    parts = strip(acquisitions, rims(acquisitions), win_rows, win_cols, groups)
    return to_slots(pair_list, parts)


def solution(mesh):
    return jax.shard_map(
        functools.partial(shards, mesh.shape["date"] // GROUP),
        mesh=mesh,
        in_specs=(P(None, "date", "grp", "tile"), P("date", None), P(), P()),
        out_specs=P(None, "date", "grp", "tile"),
        check_vma=False,
    )
```

time: 550 us -> 92.6 us (0.17)
  waiting for transfers between devices: 255 us -> 0.01 us
  local copies, waits for them, and re-layouts: 201 us -> 0.87 us
  Pallas kernels: 0 us -> 87.5 us
  other arithmetic: 46.4 us -> 1.58 us
  matrix products: 36.7 us -> 0 us
    ppermute x5 -> x1, waiting for transfers between devices: 255 us -> 0.01 us  [rims(): incoming = lax.ppermute(outgoing, 'tile', [(0, 1), (1, 0)])]
    gather x60 -> x0, local copies, waits for them, and re-layouts: 183 us -> none  [the longest x15 93.1 us: one_block(): lead_tile = jnp.take(window, first_local, axis=1).astype(jnp.float32)]
    pallas_call x0 -> x2, Pallas kernels: none -> 87.5 us  [the longest x1 81 us: strip(): pl.pallas_call(functools.partial(strip_kernel, groups, rows, width), out_...]
    dot_general x32 -> x0, matrix products: 36.7 us -> none  [the longest x15 25.3 us: one_block(): jnp.einsum('cprx,xk->cprk', product, col_taps, preferred_element_type=jnp...]
    convert_element_type x15 -> x0, other arithmetic: 33.5 us -> none  [one_block(): other_tile = jnp.take(window, second_local, axis=1).astype(jnp.float32)]
    unnamed x12 -> x5, local copies, waits for them, and re-layouts: 10.8 us -> 0.79 us
    another operation x15 -> x2, other arithmetic: 7.9 us -> 0.21 us  [rims(): return jnp.stack(pieces)]
  transfers between devices with their start and end apart: 5 -> 1, of which waited for: 4 -> 0; matrix products, arithmetic and copies ran while one was open for 1% -> 1% of each run, Pallas kernels for 0% -> 0%
where the time goes in v3:
time: 92.6 us; the launch traced here: 91.1 us
  Pallas kernels  87.5 us (94%)
  other arithmetic  1.58 us (2%)
    pallas_call x1, Pallas kernels, strip(): pl.pallas_call(functools.partial(strip_kernel, groups, rows, width), out_...  81 us
    pallas_call x1, Pallas kernels, to_slots(): pl.pallas_call(functools.partial(slots_kernel, count), out_shape=jax.Shap...  6.44 us
  transfers between devices with their start and end apart: 1, of which 0 were waited for; matrix products, arithmetic and copies ran while one was open for 1% of the time, Pallas kernels for 0%

profile of v3, /device:TPU:0, one launch (start us, length us, event | category | flops | bytes accessed | tf_op | source)
XLA Modules:
  0.0 91.1 jit_solution(1761160040440836574)
XLA Ops:
  0.0 0.0 copy-start
  0.0 0.0 copy-start.1
  0.0 1.4 %fusion = (bf16[2,4,32,8]{3,2,1,0:T(8,128)(2,1)S(1)}, bf16[2,4,32,8]{3,2,1,0:T(8,128)(2,1)S(1)}, bf16[2,4,32,8]{3,2,1,0:T(8,128)(2,1)S(1)}, bf16[2,4,32,8]{3,2,1...) fusion(bf16[2,4,32,4096]{3,2,1,0:T(8,128)(2,1)} %acq.1, ...), kind=kLoop, calls=%fused_computation.8 | loop fusion | flops 2048 | bytes 61441 | tf_op jit(solution)/shard_map/slice | solution.py:543
  1.4 0.5 collective-permute-start
  2.5 0.8 copy.5.pair_list
  3.3 0.1 pad.15.clone
  3.4 0.0 collective-permute-done
  3.4 0.2 maximum_bitcast_fusion
  3.6 0.0 copy-done
  3.7 0.0 copy-done.1
  3.7 81.0 %strip.1.parts = f32[4,82,8,128]{3,2,1,0:T(8,128)S(1)} custom-call(s32[8]{0:T(128)S(1)} %copy-done.1, s32[1]{0:T(128)S(6)} %copy.6.win_cols, bf16[2,4,32,4096]{3,2,1,0:T(8,128)(2,1)S(1)} %copy-done, bf16[4,2,4,32,128]{4,3,2,1,0:T(8,128)(2,1)S(1)} %pad_maximum_fusion.rim), custom_call_target="tpu_custom_call" | custom-call | tf_op jit(solution)/shard_map/strip/pallas_call | solution.py:450
  84.7 6.4 %to_slots.1 = f32[2,60,8,256]{3,2,1,0:T(8,128)} custom-call(s32[60,2]{1,0:T(8,128)S(1)} %copy.5.pair_list, f32[4,82,8,128]{3,2,1,0:T(8,128)S(1)} %strip.1.parts), custom_call_target="tpu_custom_call" | custom-call | tf_op jit(solution)/shard_map/to_slots/pallas_call | solution.py:518
  (3 shorter events, 0.1 us)
Async XLA Ops:
  0.0 3.6 %copy-start = (bf16[2,4,32,4096]{3,2,1,0:T(8,128)(2,1)S(1)}, bf16[2,4,32,4096]{3,2,1,0:T(8,128)(2,1)}, u32[]{:S(2)}) copy-start(bf16[2,4,32,4096]{3,2,1,0:T(8,128)(2,1)} %acq.1) | copy-start | bytes 6291460
  0.0 3.7 %copy-start.1 = (s32[8]{0:T(128)S(1)}, s32[8]{0:T(128)}, u32[]{:S(2)}) copy-start(s32[8]{0:T(128)} %win_rows.1) | copy-start | bytes 100
  1.4 2.0 %collective-permute-start = (bf16[2,4,32,8]{3,2,1,0:T(8,128)(2,1)S(1)}, bf16[2,4,32,8]{3,2,1,0:T(8,128)(2,1)S(1)}, u32[]{:S(2)}, u32[]{:S(2)}) collective-permute-start(bf16[2,4,32,8]{3,2,1,0:T(8,128)(2,1)S(1)} %get-tuple-element.9), channel_id=1, source_target_pairs={{0,1},{1,0},{2,3},{3,2},{4,5},{5,4},{6,7},{7,6},{8,9},{9,8},{10,11... | collective-permute-start | bytes 12296 | tf_op jit(solution)/shard_map/ppermute | solution.py:535

commit v4 on v3

--- a/solution.py
+++ b/solution.py
@@ -21,7 +21,8 @@
 HELD = LOCAL + DOWN + UP
 HALF = STRIDE_C // 2
 LANES = 128
-CHUNK = 24
+PART = 16
+CHUNK = 40
 MESH = pl.DeviceIdType.MESH
 
 
@@ -105,7 +106,8 @@
     out_rows = rows // STRIDE_R
     out_cols = width // STRIDE_C
     full = width + LANES
-    cuts = [(r, c) for r in range(0, rows, 16) for c in range(0, full, 384)]
+    cuts = range(0, full, 384)
+    halves = rows // PART
     date = lax.axis_index("date")
     group, member = date // GROUP, date % GROUP
     base = group * GROUP
@@ -146,14 +148,15 @@
     peers = peers + has_after.astype(jnp.int32) * (1 + 3 * late)
     pl.semaphore_wait(pltpu.get_barrier_semaphore(), peers)
 
-    def body_of(who):
-        return acq.at[:, :, :, pl.ds(pl.multiple_of(who * width, width), width)]
-
-    def rim_of(who):
-        return rim.at[who]
-
-    def slot(start, count):
-        part = held.at[:, pl.ds(start, count)]
+    def body_of(who, h):
+        columns = pl.ds(pl.multiple_of(who * width, width), width)
+        return acq.at[:, :, pl.ds(h * PART, PART), columns]
+
+    def rim_of(who, h):
+        return rim.at[who, :, :, pl.ds(h * PART, PART)]
+
+    def slot(start, count, h):
+        part = held.at[:, pl.ds(start, count), pl.ds(h * PART, PART)]
         return part.at[:, :, :, pl.ds(0, width)], part.at[:, :, :, pl.ds(width, LANES)]
 
     def remote(src, dst, send_sem, recv_sem, where):
@@ -173,49 +176,59 @@
         (3 * OWN, OWN, LOCAL + DOWN + 3 * OWN - UP_FROM, 1),
     ]
 
-    def far(source, mine):
+    def far(source, mine, h):
         start, count, place, step = onward[source]
         if mine:
             skip = start - source * OWN
-            srcs = [ref.at[:, pl.ds(skip, count)] for ref in (body_of(source), rim_of(source))]
+            refs = (body_of(source, h), rim_of(source, h))
+            srcs = [ref.at[:, pl.ds(skip, count)] for ref in refs]
         else:
-            srcs = slot(start, count)
+            srcs = slot(start, count, h)
         return [
             remote(
-                src, dst, far_send.at[source, n], far_recv.at[source, n], date + step * GROUP
+                src,
+                dst,
+                far_send.at[h, source, n],
+                far_recv.at[h, source, n],
+                date + step * GROUP,
             )
-            for n, (src, dst) in enumerate(zip(srcs, slot(place, count)))
+            for n, (src, dst) in enumerate(zip(srcs, slot(place, count, h)))
         ]
 
-    def pass_on(who, mine):
+    def pass_on(who, mine, h):
         for source in range(GROUP):
             exists = has_before if onward[source][3] < 0 else has_after
 
             @pl.when(jnp.logical_and(who == source, exists))
             def _():
-                for copy in far(source, mine):
+                for copy in far(source, mine, h):
                     copy.start()
 
-    near = []
+    def near(k, h):
+        who = other_member(member, k)
+        srcs = (body_of(who, h), rim_of(who, h))
+        return [
+            remote(src, dst, send.at[h, k, n], recv.at[h, k, n], base + who)
+            for n, (src, dst) in enumerate(zip(srcs, slot(member * OWN, OWN, h)))
+        ]
+
+    def own(h):
+        main, side = slot(member * OWN, OWN, h)
+        return [
+            pltpu.make_async_copy(body_of(member, h), main, local.at[h, 0]),
+            pltpu.make_async_copy(rim_of(member, h), side, local.at[h, 1]),
+        ]
+
+    def send_near(k, h):
+        for copy in near(k, h):
+            copy.start()
+
     for k in (1, 2, 3):
-        who = other_member(member, k)
-        pair = [
-            remote(src, dst, send.at[k, n], recv.at[k, n], base + who)
-            for n, (src, dst) in enumerate(
-                zip((body_of(who), rim_of(who)), slot(member * OWN, OWN))
-            )
-        ]
-        for copy in pair:
+        send_near(k, 0)
+    pass_on(member, True, 0)
+    for h in range(halves):
+        for copy in own(h):
             copy.start()
-        near.append(pair)
-    pass_on(member, True)
-    main, side = slot(member * OWN, OWN)
-    mine = [
-        pltpu.make_async_copy(body_of(member), main, local.at[0]),
-        pltpu.make_async_copy(rim_of(member), side, local.at[1]),
-    ]
-    for copy in mine:
-        copy.start()
 
     lane = lax.broadcasted_iota(jnp.int32, (full, LANES), 0)
     out = lax.broadcasted_iota(jnp.int32, (full, LANES), 1) % out_cols
@@ -225,74 +238,88 @@
     beside = jnp.abs(2 * column + 1 - (2 * out + 1) * STRIDE_C) <= win_cols[0]
     beside = jnp.logical_and(beside, lane < width + 2 * HALF)
     col_taps[...] = jnp.where(beside, 1.0, 0.0).astype(jnp.bfloat16)
-    shape = (CHUNK * out_rows, CHUNK * rows)
+    shape = (CHUNK * out_rows, CHUNK * PART)
     at = lax.broadcasted_iota(jnp.int32, shape, 0)
     row = lax.broadcasted_iota(jnp.int32, shape, 1)
     window = jnp.zeros(shape, jnp.int32)
     for o in range(out_rows):
         window = jnp.where(at % out_rows == o, win_rows[o], window)
-    inside = jnp.abs(2 * (row % rows) + 1 - (2 * (at % out_rows) + 1) * STRIDE_R) <= window
-    inside = jnp.logical_and(inside, at // out_rows == row // rows)
-    row_taps[...] = jnp.where(inside, 1.0, 0.0).astype(jnp.bfloat16)
-
-    def widen(start, count, shift):
+    same = at // out_rows == row // PART
+    for h in range(halves):
+        reach = 2 * (row % PART + h * PART) + 1 - (2 * (at % out_rows) + 1) * STRIDE_R
+        inside = jnp.logical_and(jnp.abs(reach) <= window, same)
+        row_taps[h] = jnp.where(inside, 1.0, 0.0).astype(jnp.bfloat16)
+
+    def widen(start, count, shift, h):
+        low, high = h * PART, (h + 1) * PART
+
         def one_date(n, carry):
             d = start + n
-            for r, c in cuts:
-                re = held[0, d, r : r + 16, c : c + 384].astype(jnp.float32)
-                im = held[1, d, r : r + 16, c : c + 384].astype(jnp.float32)
-                wide[0, d, r : r + 16, c : c + 384] = re
-                wide[1, d, r : r + 16, c : c + 384] = im
-                to = pl.multiple_of((d - shift) * rows + r, 16)
-                product[pl.ds(to, 16), c : c + 384] = (re * re + im * im).astype(jnp.bfloat16)
+            for c in cuts:
+                re = held[0, d, low:high, c : c + 384].astype(jnp.float32)
+                im = held[1, d, low:high, c : c + 384].astype(jnp.float32)
+                wide[0, d, low:high, c : c + 384] = re
+                wide[1, d, low:high, c : c + 384] = im
+                to = pl.multiple_of((d - shift) * PART, PART)
+                product[pl.ds(to, PART), c : c + 384] = (re * re + im * im).astype(jnp.bfloat16)
             return carry
 
         lax.fori_loop(0, count, one_date, 0)
 
-    def blank(start, count, shift):
+    def blank(start, count, shift, h):
         def one_date(n, carry):
             d = start + n
             for part in range(2):
-                wide[part, d] = jnp.zeros((rows, full), jnp.float32)
-            to = pl.multiple_of((d - shift) * rows, 16)
-            product[pl.ds(to, rows), :] = jnp.zeros((rows, full), jnp.bfloat16)
+                wide[part, d, h * PART : (h + 1) * PART] = jnp.zeros((PART, full), jnp.float32)
+            to = pl.multiple_of((d - shift) * PART, PART)
+            product[pl.ds(to, PART), :] = jnp.zeros((PART, full), jnp.bfloat16)
             return carry
 
         lax.fori_loop(0, count, one_date, 0)
 
-    def look_power(start):
+    def look_power(start, h):
         across = jnp.dot(
-            product[: LOCAL * rows], col_taps[...], preferred_element_type=jnp.float32
+            product[: LOCAL * PART], col_taps[...], preferred_element_type=jnp.float32
         )
-        taps = row_taps[: LOCAL * out_rows, : LOCAL * rows]
-        power[start : start + LOCAL] = split_dot(taps, across).reshape(LOCAL, out_rows, LANES)
-
-    def work(total, pair_of):
+        taps = row_taps[h, : LOCAL * out_rows, : LOCAL * PART]
+        sums = split_dot(taps, across).reshape(LOCAL, out_rows, LANES)
+        if h:
+            sums = sums + power[start : start + LOCAL]
+        power[start : start + LOCAL] = sums
+
+    def work(total, pair_of, h):
+        low, high = h * PART, (h + 1) * PART
+
         def one_chunk(chunk, carry):
             def one_pair(p, carry):
                 i, j, _ = pair_of(chunk * CHUNK + p)
-                for r, c in cuts:
-                    re_i = wide[0, i, r : r + 16, c : c + 384]
-                    im_i = wide[1, i, r : r + 16, c : c + 384]
-                    re_j = wide[0, j, r : r + 16, c : c + 384]
-                    im_j = wide[1, j, r : r + 16, c : c + 384]
+                to = pl.multiple_of(p * 2 * PART, 2 * PART)
+                for c in cuts:
+                    re_i = wide[0, i, low:high, c : c + 384]
+                    im_i = wide[1, i, low:high, c : c + 384]
+                    re_j = wide[0, j, low:high, c : c + 384]
+                    im_j = wide[1, j, low:high, c : c + 384]
                     re = (re_i * re_j + im_i * im_j).astype(jnp.bfloat16)
                     im = (im_i * re_j - re_i * im_j).astype(jnp.bfloat16)
-                    product[pl.ds(pl.multiple_of(p * 2 * rows + r, 16), 16), c : c + 384] = re
-                    at = pl.multiple_of(p * 2 * rows + rows + r, 16)
-                    product[pl.ds(at, 16), c : c + 384] = im
+                    product[pl.ds(to, PART), c : c + 384] = re
+                    product[pl.ds(to + PART, PART), c : c + 384] = im
                 return carry
 
             lax.fori_loop(0, CHUNK, one_pair, 0)
             across = jnp.dot(product[...], col_taps[...], preferred_element_type=jnp.float32)
-            across = across.reshape(CHUNK, 2, rows, LANES)
-            left = lax.broadcasted_iota(jnp.int32, (CHUNK, rows, LANES), 2) < out_cols
-            both = jnp.where(left, across[:, 0], across[:, 1]).reshape(CHUNK * rows, LANES)
-            looked[...] = split_dot(row_taps[...], both).reshape(CHUNK, out_rows, LANES)
+            across = across.reshape(CHUNK, 2, PART, LANES)
+            left = lax.broadcasted_iota(jnp.int32, (CHUNK, PART, LANES), 2) < out_cols
+            both = jnp.where(left, across[:, 0], across[:, 1]).reshape(CHUNK * PART, LANES)
+            looked[...] = split_dot(row_taps[h], both).reshape(CHUNK, out_rows, LANES)
 
             def finish(p, carry):
                 i, j, to = pair_of(chunk * CHUNK + p)
-                outbox[to] = looked[p] * lax.rsqrt(power[i] * power[j] + EPS)
+                sums = looked[p]
+                if h:
+                    sums = sums + outbox[to]
+                if h == halves - 1:
+                    sums = sums * lax.rsqrt(power[i] * power[j] + EPS)
+                outbox[to] = sums
                 return carry
 
             lax.fori_loop(0, CHUNK, finish, 0)
@@ -375,35 +402,50 @@
             base - GROUP + target,
         )
 
-    for copy in mine:
-        copy.wait()
-    widen(member * OWN, OWN, 0)
-    for k in (1, 2, 3):
-        for copy in near[k - 1]:
-            copy.wait_recv()
-        who = other_member(member, k)
-        pass_on(who, False)
-        widen(who * OWN, OWN, 0)
-    look_power(0)
-    work(INSIDE, inside_pair)
+    def take_near(h):
+        for copy in own(h):
+            copy.wait()
+        widen(member * OWN, OWN, 0, h)
+        for k in (1, 2, 3):
+            for copy in near(k, h):
+                copy.wait_recv()
+            who = other_member(member, k)
+            pass_on(who, False, h)
+            if h + 1 < halves:
+                send_near(k, h + 1)
+            widen(who * OWN, OWN, 0, h)
+        if h + 1 < halves:
+            pass_on(member, True, h + 1)
+        look_power(0, h)
+
+    def take_far(h):
+        for source in range(GROUP):
+            start, count, place, step = onward[source]
+            gets = has_after if step < 0 else has_before
+
+            @pl.when(gets)
+            def _():
+                for copy in far(source, False, h):
+                    copy.wait_recv()
+                widen(place, count, LOCAL, h)
+
+            @pl.when(jnp.logical_not(gets))
+            def _():
+                blank(place, count, LOCAL, h)
+
+        look_power(LOCAL, h)
+
+    across_total = RECT + 2 * FOLD
+    take_near(0)
+    work(INSIDE, inside_pair, 0)
+    for h in range(1, halves):
+        take_near(h)
+        take_far(h - 1)
+        work(across_total, cross_pair, h - 1)
+        work(INSIDE, inside_pair, h)
     give_back(0)
-
-    for source in range(GROUP):
-        start, count, place, step = onward[source]
-        gets = has_after if step < 0 else has_before
-
-        @pl.when(gets)
-        def _():
-            for copy in far(source, False):
-                copy.wait_recv()
-            widen(place, count, LOCAL)
-
-        @pl.when(jnp.logical_not(gets))
-        def _():
-            blank(place, count, LOCAL)
-
-    look_power(LOCAL)
-    work(RECT + 2 * FOLD, cross_pair)
+    take_far(halves - 1)
+    work(across_total, cross_pair, halves - 1)
     give_back(1)
 
     @pl.when(has_before)
@@ -411,16 +453,17 @@
         for target in (2, 3):
             up_copy(member, target).start()
 
-    for pair in near:
-        for copy in pair:
-            copy.wait_send()
-    for source in range(GROUP):
-        exists = has_before if onward[source][3] < 0 else has_after
-
-        @pl.when(exists)
-        def _():
-            for copy in far(source, False):
+    for h in range(halves):
+        for k in (1, 2, 3):
+            for copy in near(k, h):
                 copy.wait_send()
+        for source in range(GROUP):
+            exists = has_before if onward[source][3] < 0 else has_after
+
+            @pl.when(exists)
+            def _():
+                for copy in far(source, False, h):
+                    copy.wait_send()
 
     end_back(0)
     end_back(1)
@@ -444,6 +487,7 @@
     full = width + LANES
     out_rows = rows // STRIDE_R
     dates = (2, HELD, rows, full)
+    halves = rows // PART
     smem = pl.BlockSpec(memory_space=pltpu.SMEM)
     hbm = pl.BlockSpec(memory_space=pl.ANY)
     dma = pltpu.SemaphoreType.DMA
@@ -457,17 +501,17 @@
         scratch_shapes=[
             pltpu.VMEM(dates, acq.dtype),
             pltpu.VMEM(dates, jnp.float32),
-            pltpu.VMEM((2 * CHUNK * rows, full), jnp.bfloat16),
+            pltpu.VMEM((2 * CHUNK * PART, full), jnp.bfloat16),
             pltpu.VMEM((full, LANES), jnp.bfloat16),
-            pltpu.VMEM((CHUNK * out_rows, CHUNK * rows), jnp.bfloat16),
+            pltpu.VMEM((halves, CHUNK * out_rows, CHUNK * PART), jnp.bfloat16),
             pltpu.VMEM((2 * LOCAL, out_rows, LANES), jnp.float32),
             pltpu.VMEM((CHUNK, out_rows, LANES), jnp.float32),
             pltpu.VMEM((OUTBOX + FOLD, out_rows, LANES), jnp.float32),
-            dma((GROUP, 2)),
-            dma((GROUP, 2)),
-            dma((GROUP, 2)),
-            dma((GROUP, 2)),
-            dma((2,)),
+            dma((halves, GROUP, 2)),
+            dma((halves, GROUP, 2)),
+            dma((halves, GROUP, 2)),
+            dma((halves, GROUP, 2)),
+            dma((halves, 2)),
             dma((2, GROUP, OWN)),
             dma((2, GROUP, OWN)),
             dma((GROUP,)),

time: 92.6 us -> 97.9 us (1.057)
  Pallas kernels: 87.5 us -> 92.9 us
    pallas_call x1, Pallas kernels: 81 us -> 86.5 us  [strip(): pl.pallas_call(functools.partial(strip_kernel, groups, rows, width), out_...]
where the time goes in v4:
time: 97.9 us; the launch traced here: 96.6 us
  Pallas kernels  92.9 us (95%)
  other arithmetic  1.58 us (2%)
    pallas_call x1, Pallas kernels, strip(): pl.pallas_call(functools.partial(strip_kernel, groups, rows, width), out_...  86.5 us
    pallas_call x1, Pallas kernels, to_slots(): pl.pallas_call(functools.partial(slots_kernel, count), out_shape=jax.Shap...  6.44 us
  transfers between devices with their start and end apart: 1, of which 0 were waited for; matrix products, arithmetic and copies ran while one was open for 1% of the time, Pallas kernels for 0%

profile of v4, /device:TPU:0, one launch (start us, length us, event | category | flops | bytes accessed | tf_op | source)
XLA Modules:
  0.0 96.6 jit_solution(6843525791962128646)
XLA Ops:
  0.0 0.0 copy-start
  0.0 0.0 copy-start.1
  0.0 1.4 %fusion = (bf16[2,4,32,8]{3,2,1,0:T(8,128)(2,1)S(1)}, bf16[2,4,32,8]{3,2,1,0:T(8,128)(2,1)S(1)}, bf16[2,4,32,8]{3,2,1,0:T(8,128)(2,1)S(1)}, bf16[2,4,32,8]{3,2,1...) fusion(bf16[2,4,32,4096]{3,2,1,0:T(8,128)(2,1)} %acq.1, ...), kind=kLoop, calls=%fused_computation.8 | loop fusion | flops 2048 | bytes 61441 | tf_op jit(solution)/shard_map/slice | solution.py:587
  1.4 0.5 collective-permute-start
  2.5 0.8 copy.5.pair_list
  3.3 0.1 pad.15.clone
  3.4 0.0 collective-permute-done
  3.4 0.2 maximum_bitcast_fusion
  3.6 0.0 copy-done
  3.7 0.0 copy-done.1
  3.7 86.5 %strip.1.parts = f32[4,82,8,128]{3,2,1,0:T(8,128)S(1)} custom-call(s32[8]{0:T(128)S(1)} %copy-done.1, s32[1]{0:T(128)S(6)} %copy.6.win_cols, bf16[2,4,32,4096]{3,2,1,0:T(8,128)(2,1)S(1)} %copy-done, bf16[4,2,4,32,128]{4,3,2,1,0:T(8,128)(2,1)S(1)} %pad_maximum_fusion.rim), custom_call_target="tpu_custom_call" | custom-call | tf_op jit(solution)/shard_map/strip/pallas_call | solution.py:494
  90.1 6.4 %to_slots.1 = f32[2,60,8,256]{3,2,1,0:T(8,128)} custom-call(s32[60,2]{1,0:T(8,128)S(1)} %copy.5.pair_list, f32[4,82,8,128]{3,2,1,0:T(8,128)S(1)} %strip.1.parts), custom_call_target="tpu_custom_call" | custom-call | tf_op jit(solution)/shard_map/to_slots/pallas_call | solution.py:562
  (3 shorter events, 0.1 us)
Async XLA Ops:
  0.0 3.6 %copy-start = (bf16[2,4,32,4096]{3,2,1,0:T(8,128)(2,1)S(1)}, bf16[2,4,32,4096]{3,2,1,0:T(8,128)(2,1)}, u32[]{:S(2)}) copy-start(bf16[2,4,32,4096]{3,2,1,0:T(8,128)(2,1)} %acq.1) | copy-start | bytes 6291460
  0.0 3.7 %copy-start.1 = (s32[8]{0:T(128)S(1)}, s32[8]{0:T(128)}, u32[]{:S(2)}) copy-start(s32[8]{0:T(128)} %win_rows.1) | copy-start | bytes 100
  1.4 2.0 %collective-permute-start = (bf16[2,4,32,8]{3,2,1,0:T(8,128)(2,1)S(1)}, bf16[2,4,32,8]{3,2,1,0:T(8,128)(2,1)S(1)}, u32[]{:S(2)}, u32[]{:S(2)}) collective-permute-start(bf16[2,4,32,8]{3,2,1,0:T(8,128)(2,1)S(1)} %get-tuple-element.9), channel_id=1, source_target_pairs={{0,1},{1,0},{2,3},{3,2},{4,5},{5,4},{6,7},{7,6},{8,9},{9,8},{10,11... | collective-permute-start | bytes 12296 | tf_op jit(solution)/shard_map/ppermute | solution.py:579

commit v5 on v3

--- a/solution.py
+++ b/solution.py
@@ -283,7 +283,7 @@
                     product[pl.ds(at, 16), c : c + 384] = im
                 return carry
 
-            lax.fori_loop(0, CHUNK, one_pair, 0)
+            lax.fori_loop(0, CHUNK, one_pair, 0, unroll=2)
             across = jnp.dot(product[...], col_taps[...], preferred_element_type=jnp.float32)
             across = across.reshape(CHUNK, 2, rows, LANES)
             left = lax.broadcasted_iota(jnp.int32, (CHUNK, rows, LANES), 2) < out_cols
@@ -295,7 +295,7 @@
                 outbox[to] = looked[p] * lax.rsqrt(power[i] * power[j] + EPS)
                 return carry
 
-            lax.fori_loop(0, CHUNK, finish, 0)
+            lax.fori_loop(0, CHUNK, finish, 0, unroll=8)
             return carry
 
         lax.fori_loop(0, total // CHUNK, one_chunk, 0)
@@ -508,7 +508,7 @@
             out[1, s, :, n * LANES : (n + 1) * LANES] = jnp.where(alive, im, 0.0)
         return carry
 
-    lax.fori_loop(0, count, one_slot, 0)
+    lax.fori_loop(0, count, one_slot, 0, unroll=6)
 
 
 def to_slots(pair_list, parts):

time: 92.6 us -> 84.1 us (0.908)
  Pallas kernels: 87.5 us -> 79 us
    pallas_call x1, Pallas kernels: 81 us -> 75.5 us  [strip(): pl.pallas_call(functools.partial(strip_kernel, groups, rows, width), out_...]
    pallas_call x1, Pallas kernels: 6.44 us -> 3.43 us  [to_slots(): pl.pallas_call(functools.partial(slots_kernel, count), out_shape=jax.Shap...]
where the time goes in v5:
time: 84.1 us; the launch traced here: 82.6 us
  Pallas kernels  79 us (94%)
  other arithmetic  1.58 us (2%)
  local copies, waits for them, and re-layouts  0.87 us (1%)
    pallas_call x1, Pallas kernels, strip(): pl.pallas_call(functools.partial(strip_kernel, groups, rows, width), out_...  75.5 us
    pallas_call x1, Pallas kernels, to_slots(): pl.pallas_call(functools.partial(slots_kernel, count), out_shape=jax.Shap...  3.43 us
  transfers between devices with their start and end apart: 1, of which 0 were waited for; matrix products, arithmetic and copies ran while one was open for 1% of the time, Pallas kernels for 0%

profile of v5, /device:TPU:0, one launch (start us, length us, event | category | flops | bytes accessed | tf_op | source)
XLA Modules:
  0.0 82.6 jit_solution(6741024660702650953)
XLA Ops:
  0.0 0.0 copy-start
  0.0 0.0 copy-start.1
  0.0 1.4 %fusion = (bf16[2,4,32,8]{3,2,1,0:T(8,128)(2,1)S(1)}, bf16[2,4,32,8]{3,2,1,0:T(8,128)(2,1)S(1)}, bf16[2,4,32,8]{3,2,1,0:T(8,128)(2,1)S(1)}, bf16[2,4,32,8]{3,2,1...) fusion(bf16[2,4,32,4096]{3,2,1,0:T(8,128)(2,1)} %acq.1, ...), kind=kLoop, calls=%fused_computation.8 | loop fusion | flops 2048 | bytes 61441 | tf_op jit(solution)/shard_map/slice | solution.py:543
  1.4 0.5 collective-permute-start
  2.5 0.8 copy.5.pair_list
  3.3 0.1 pad.15.clone
  3.4 0.0 collective-permute-done
  3.4 0.2 maximum_bitcast_fusion
  3.6 0.0 copy-done
  3.7 0.0 copy-done.1
  3.7 75.5 %strip.1.parts = f32[4,82,8,128]{3,2,1,0:T(8,128)S(1)} custom-call(s32[8]{0:T(128)S(1)} %copy-done.1, s32[1]{0:T(128)S(6)} %copy.6.win_cols, bf16[2,4,32,4096]{3,2,1,0:T(8,128)(2,1)S(1)} %copy-done, bf16[4,2,4,32,128]{4,3,2,1,0:T(8,128)(2,1)S(1)} %pad_maximum_fusion.rim), custom_call_target="tpu_custom_call" | custom-call | tf_op jit(solution)/shard_map/strip/pallas_call | solution.py:450
  79.2 3.4 %to_slots.1 = f32[2,60,8,256]{3,2,1,0:T(8,128)} custom-call(s32[60,2]{1,0:T(8,128)S(1)} %copy.5.pair_list, f32[4,82,8,128]{3,2,1,0:T(8,128)S(1)} %strip.1.parts), custom_call_target="tpu_custom_call" | custom-call | tf_op jit(solution)/shard_map/to_slots/pallas_call | solution.py:518
  (3 shorter events, 0.1 us)
Async XLA Ops:
  0.0 3.6 %copy-start = (bf16[2,4,32,4096]{3,2,1,0:T(8,128)(2,1)S(1)}, bf16[2,4,32,4096]{3,2,1,0:T(8,128)(2,1)}, u32[]{:S(2)}) copy-start(bf16[2,4,32,4096]{3,2,1,0:T(8,128)(2,1)} %acq.1) | copy-start | bytes 6291460
  0.0 3.7 %copy-start.1 = (s32[8]{0:T(128)S(1)}, s32[8]{0:T(128)}, u32[]{:S(2)}) copy-start(s32[8]{0:T(128)} %win_rows.1) | copy-start | bytes 100
  1.4 2.0 %collective-permute-start = (bf16[2,4,32,8]{3,2,1,0:T(8,128)(2,1)S(1)}, bf16[2,4,32,8]{3,2,1,0:T(8,128)(2,1)S(1)}, u32[]{:S(2)}, u32[]{:S(2)}) collective-permute-start(bf16[2,4,32,8]{3,2,1,0:T(8,128)(2,1)S(1)} %get-tuple-element.9), channel_id=1, source_target_pairs={{0,1},{1,0},{2,3},{3,2},{4,5},{5,4},{6,7},{7,6},{8,9},{9,8},{10,11... | collective-permute-start | bytes 12296 | tf_op jit(solution)/shard_map/ppermute | solution.py:535
